TPU v7x, 1024 devices: a whole 4x8x16 slice. The times are simulated.
1024 devices in a mesh: depth: 16 (over y, core), row: 8 (over x, z_hi), col: 8 (over z_lo).
Axes of the slice: x: 4, y: 8, z: 16 (z_hi: 2, z_lo: 8; z = z_hi * 8 + z_lo), core: 2. Of those that a mesh axis runs over, the one named last changes fastest.
Arguments:
- act_values: bfloat16 [2048, 4096], P('depth', 'row'), may hold values from -6 to 6
- activation_scale: float32 [2048, 32], P('depth', 'row'), may hold values from 0.25 to 4
- token_order: int32 [16, 128], P('depth'), may hold values from 0 to 127, each once within a row
- gate_q: bfloat16 [4096, 14336], P('row', 'col'), may hold values from -0.09375 to 0.09375
- gate_scale: float32 [32, 112], P('row', 'col'), may hold values from 0.5 to 2
- up_q: bfloat16 [4096, 14336], P('row', 'col'), may hold values from -0.09375 to 0.09375
- up_scale: float32 [32, 112], P('row', 'col'), may hold values from 0.5 to 2
- cotangent: bfloat16 [2048, 14336], P(('depth', 'row'), 'col'), may hold values from -5 to 5
Outputs:
- grad_act: bfloat16 [2048, 4096], P(('depth', 'col'), 'row')
- grad_gate: bfloat16 [4096, 14336], P('row', ('col', 'depth'))
- grad_up: bfloat16 [4096, 14336], P('row', ('col', 'depth'))
Inputs may be any that keep to these rules, and one draw needn't show every extreme that they name: Each row of token_order is a permutation of 0 to 127.
All inputs are finite; a program needn't handle non-finite values.
Results may differ from a plain program's by a relative error of at most 0.033.
Values may be sent and summed in bfloat16 or wider, within the bound.
No kernel may reach another device: no remote copies, remote signals or barrier semaphores. Data moves between devices by JAX's collectives and lax.ppermute only.
A program may use at most 32 MiB of HBM per device.

v0:
```python
import jax
import jax.numpy as jnp
from jax import lax
from jax.sharding import PartitionSpec as P

GROUP = 128


def dequant_block(values, scales, group_side):
    height, width = values.shape
    blocks = (
        values.astype(jnp.float32).reshape(
            height // group_side, group_side, width // group_side, group_side
        )
        * scales[:, None, :, None]
    )
    return blocks.reshape(height, width).astype(jnp.bfloat16)


def on_device(
    act_values, activation_scale, token_order, gate_q, gate_scale, up_q, up_scale, cotangent
):
    depth_count = lax.axis_size("depth")
    local_tok, local_feat = act_values.shape
    groups = activation_scale.shape[1]
    scaled = (
        (
            act_values.astype(jnp.float32).reshape(local_tok, groups, local_feat // groups)
            * activation_scale[:, :, None]
        )
        .reshape(local_tok, local_feat)
        .astype(jnp.bfloat16)
    )
    one_hot_matrix = (
        token_order[0][None, :] == jnp.arange(local_tok, dtype=jnp.int32)[:, None]
    ).astype(jnp.bfloat16)
    natural_order = jnp.dot(one_hot_matrix, scaled, preferred_element_type=jnp.float32).astype(
        jnp.bfloat16
    )
    gate_weight = dequant_block(gate_q, gate_scale, GROUP)
    w_up = dequant_block(up_q, up_scale, GROUP)
    feat_rows, hid_cols = gate_weight.shape
    slice_width = hid_cols // depth_count
    w_both = jnp.concatenate(
        [
            gate_weight.reshape(feat_rows, depth_count, slice_width),
            w_up.reshape(feat_rows, depth_count, slice_width),
        ],
        axis=2,
    ).reshape(feat_rows, 2 * hid_cols)
    summed = lax.psum_scatter(
        jnp.dot(natural_order, w_both, preferred_element_type=jnp.float32).astype(jnp.bfloat16),
        "row",
        scatter_dimension=0,
        tiled=True,
    ).astype(jnp.float32)
    own_rows = summed.shape[0]
    paired = summed.reshape(own_rows, depth_count, 2 * slice_width)
    gate_pre = paired[:, :, :slice_width]
    up_pre = paired[:, :, slice_width:]
    slope_in = cotangent.astype(jnp.float32).reshape(own_rows, depth_count, slice_width)
    sigmoid_gate = jax.nn.sigmoid(gate_pre)
    d_gate = (slope_in * up_pre * sigmoid_gate * (1.0 + gate_pre * (1.0 - sigmoid_gate))).astype(
        jnp.bfloat16
    )
    d_up = (slope_in * gate_pre * sigmoid_gate).astype(jnp.bfloat16)
    d_both = jnp.concatenate([d_gate, d_up], axis=2).reshape(own_rows, 2 * hid_cols)
    d_rows = lax.all_gather(d_both, "row", axis=0, tiled=True)
    picked = d_rows
    grad_act = lax.psum_scatter(
        lax.dot_general(
            picked, w_both, (((1,), (1,)), ((), ())), preferred_element_type=jnp.float32
        ).astype(jnp.bfloat16),
        "col",
        scatter_dimension=0,
        tiled=True,
    )
    picked = d_rows
    owned_rows = lax.psum_scatter(
        lax.dot_general(
            picked, natural_order, (((0,), (0,)), ((), ())), preferred_element_type=jnp.float32
        ).astype(jnp.bfloat16),
        "depth",
        scatter_dimension=0,
        tiled=True,
    ).astype(jnp.float32)
    grad_gate = owned_rows[:slice_width].T.astype(jnp.bfloat16)
    grad_up = owned_rows[slice_width:].T.astype(jnp.bfloat16)
    return (grad_act, grad_gate, grad_up)


def solution(mesh):
    return jax.shard_map(
        on_device,
        mesh=mesh,
        in_specs=(
            P("depth", "row"),
            P("depth", "row"),
            P("depth", None),
            P("row", "col"),
            P("row", "col"),
            P("row", "col"),
            P("row", "col"),
            P(("depth", "row"), "col"),
        ),
        out_specs=(
            P(("depth", "col"), "row"),
            P("row", ("col", "depth")),
            P("row", ("col", "depth")),
        ),
        check_vma=False,
    )
```

profile of v0, /device:TPU:2, one launch (start us, length us, event | category | flops | bytes accessed | tf_op | source)
XLA Modules:
  0.0 397.0 jit_solution(7870238260547315449)
XLA Ops:
  7.2 0.0 copy-start.4
  7.2 0.0 reduce-scatter.4.cloned.1.call-start
  7.2 0.8 copy.12
  8.0 0.8 copy.16
  8.8 3.8 copy.15
  12.6 0.0 copy-done.4
  12.6 0.1 copy.14
  12.7 2.8 copy.13
  15.5 0.0 copy-start.1
  15.5 0.5 mul.57
  16.1 0.9 copy-done.1
  17.0 0.7 fusion
  17.8 0.5 mul.54
  18.3 0.7 fusion.1
  19.1 0.0 copy-start.2
  19.1 0.0 copy-start.5
  19.1 0.3 pad_maximum_fusion
  19.4 0.0 copy-start
  19.4 0.0 copy-start.3
  19.4 0.2 mul.51
  19.6 0.3 copy-done.2
  20.0 0.0 copy-done.5
  20.0 0.2 convolution_convert_fusion.3
  20.2 1.1 copy-done
  21.2 2.3 convolution_convert_fusion.1
  23.5 0.0 reduce-scatter.4.cloned.1.call-update
  23.5 0.0 reduce-scatter.8.cloned.1.call-start
  23.5 0.0 copy-done.3
  23.5 0.1 reshape.51
  23.7 131.2 %reduce-scatter.4.cloned.1.call-done = bf16[16,3584]{1,0:T(8,128)(2,1)} async-done(((bf16[128,3584]{1,0:T(8,128)(2,1)}), bf16[16,3584]{1,0:T(8,128)(2,1)}) %reduce-scatter.4.cloned.1.call-update) | async-done | bytes 114704 | tf_op jit(solution)/shard_map/reduce_scatter | solution.py:51
  154.9 1.1 reshape.53
  156.0 0.1 fusion.6
  156.1 0.1 pad_maximum_fusion.1
  156.2 0.2 reshape.49
  156.4 90.2 %all_gather.3 = bf16[128,3584]{1,0:T(8,128)(2,1)S(1)} all-gather(bf16[16,3584]{1,0:T(8,128)(2,1)S(1)} %reshape.49), channel_id=1, replica_groups=mesh['depth'=16,'row'=8,'col'=8] {'row'}, dimensions={0}, use_global_device_ids=true | all-gather | bytes 1032192 | tf_op jit(solution)/shard_map/all_gather | solution.py:68
  246.6 3.0 convolution_convert_fusion
  249.5 0.0 reduce-scatter.8.cloned.1.call-update
  249.6 0.0 reduce-scatter.6.cloned.1.call-start
  249.6 3.3 convolution_convert_fusion.2
  253.0 0.0 reduce-scatter.6.cloned.1.call-update
  253.0 67.3 %reduce-scatter.8.cloned.1.call-done = bf16[224,512]{1,0:T(8,128)(2,1)} async-done(((bf16[3584,512]{1,0:T(8,128)(2,1)}), bf16[224,512]{1,0:T(8,128)(2,1)}) %reduce-scatter.8.cloned.1.call-update) | async-done | bytes 229392 | tf_op jit(solution)/shard_map/reduce_scatter | solution.py:79
  320.2 1.7 slice_bitcast_fusion
  321.9 68.6 %reduce-scatter.6.cloned.1.call-done = bf16[16,512]{1,0:T(8,128)(2,1)} async-done(((bf16[128,512]{1,0:T(8,128)(2,1)}), bf16[16,512]{1,0:T(8,128)(2,1)}) %reduce-scatter.6.cloned.1.call-update) | async-done | bytes 16400 | tf_op jit(solution)/shard_map/reduce_scatter | solution.py:70
Async XLA Ops:
  7.2 5.4 %copy-start.4 = (f32[4,14]{1,0:T(4,128)S(1)}, f32[4,14]{1,0:T(4,128)}, u32[]{:S(2)}) copy-start(f32[4,14]{1,0:T(4,128)} %param.12) | copy-start | bytes 676
  7.2 147.8 %reduce-scatter.4.cloned.1.call-start = ((), (), s32[]{:S(2)}) async-start(), calls=%async_computation.3 | async-start | bytes 1032192 | tf_op jit(solution)/shard_map/reduce_scatter | solution.py:51
  15.5 1.5 copy-start.1
  19.1 0.9 copy-start.2
  19.1 0.9 copy-start.5
  19.4 1.8 copy-start
  19.4 4.1 %copy-start.3 = (bf16[16,1792]{1,0:T(8,128)(2,1)S(1)}, bf16[16,1792]{1,0:T(8,128)(2,1)}, u32[]{:S(2)}) copy-start(bf16[16,1792]{1,0:T(8,128)(2,1)} %param.15) | copy-start | bytes 172036
  23.5 296.8 %reduce-scatter.8.cloned.1.call-start = ((), (), s32[]{:S(2)}) async-start(), calls=%async_computation.5 | async-start | bytes 3899392 | tf_op jit(solution)/shard_map/reduce_scatter | solution.py:79
  249.6 140.9 %reduce-scatter.6.cloned.1.call-start = ((), (), s32[]{:S(2)}) async-start(), calls=%async_computation.4 | async-start | bytes 147456 | tf_op jit(solution)/shard_map/reduce_scatter | solution.py:70
Sparse Core Ops, SparseCore 0:
  23.6 131.2 reduce-scatter.3
  249.7 70.5 reduce-scatter.7
  324.2 66.2 reduce-scatter.5
where the time goes:
time: 397 us
  waiting for transfers between devices  267 us (67%)
  blocking collectives  90.2 us (23%)
  local copies, waits for them, and re-layouts  14.9 us (4%)
  between operations  13.9 us (4%)
  matrix products  8.72 us (2%)
    reduce_scatter x1, waiting for transfers between devices, on_device(): lax.psum_scatter(jnp.dot(natural_order, w_both, preferred_element_type=jn...  131 us
    all_gather x1, blocking collectives, on_device(): d_rows = lax.all_gather(d_both, 'row', axis=0, tiled=True)  90.2 us
    reduce_scatter x1, waiting for transfers between devices, on_device(): lax.psum_scatter(lax.dot_general(picked, w_both, (((1,), (1,)), ((), ()))...  68.6 us
    reduce_scatter x1, waiting for transfers between devices, on_device(): lax.psum_scatter(lax.dot_general(picked, natural_order, (((0,), (0,)), ((...  67.3 us
    unnamed x17, local copies, waits for them, and re-layouts  10.6 us
  transfers between devices with their start and end apart: 3, of which 3 were waited for; matrix products, arithmetic and copies ran while one was open for 1% of the time, Pallas kernels for 0%

commit v1 on v0

v1 whole, which is shorter than its diff:
```python
import functools

import jax
import jax.numpy as jnp
from jax import lax
from jax.experimental import pallas as pl
from jax.experimental.pallas import tpu as pltpu
from jax.sharding import Mesh
from jax.sharding import PartitionSpec as P

GROUP = 128
CHUNK = 256
F32 = jnp.float32
BF16 = jnp.bfloat16


def dequant(q_ref, s_ref, first_group):
    rows = []
    for r in range(q_ref.shape[0] // GROUP):
        tiles = []
        for h in range(CHUNK // GROUP):
            tile = q_ref[r * GROUP : (r + 1) * GROUP, h * GROUP : (h + 1) * GROUP].astype(F32)
            tiles.append((tile * s_ref[r, first_group + h]).astype(BF16))
        rows.append(jnp.concatenate(tiles, axis=1))
    return jnp.concatenate(rows, axis=0)


def forward_kernel(gs_ref, us_ref, act_ref, ast_ref, order_ref, gq_ref, uq_ref, pre_ref, nat_ref):
    j = pl.program_id(0)
    tok, feat = act_ref.shape

    @pl.when(j == 0)
    def _():
        one_hot = (
            lax.broadcasted_iota(jnp.int32, (tok, tok), 0)
            == jnp.broadcast_to(order_ref[...], (tok, tok))
        ).astype(F32).astype(BF16)
        parts = []
        for g in range(feat // GROUP):
            scale = jnp.broadcast_to(ast_ref[g : g + 1, :], (tok, tok)).T
            part = act_ref[:, g * GROUP : (g + 1) * GROUP].astype(F32) * scale
            parts.append(part.astype(BF16))
        scaled = jnp.concatenate(parts, axis=1)
        nat_ref[...] = jnp.dot(one_hot, scaled, preferred_element_type=F32).astype(BF16)

    natural = nat_ref[...]
    for t, (q_ref, s_ref) in enumerate(((gq_ref, gs_ref), (uq_ref, us_ref))):
        w = dequant(q_ref, s_ref, j * (CHUNK // GROUP))
        out = jnp.dot(natural, w, preferred_element_type=F32).astype(BF16)
        pre_ref[:, 0, t] = out.reshape(pre_ref.shape[0], pre_ref.shape[3], CHUNK)


def activation_kernel(where_ref, pre_ref, own_ref, other_ref, d_ref, dp_ref, dg_ref, du_ref):
    first = where_ref[1] == 0
    n_chunks = pre_ref.shape[1]
    for j in range(n_chunks):
        cols = slice(j * CHUNK, (j + 1) * CHUNK)
        own, other = own_ref[:, cols].astype(F32), other_ref[:, cols].astype(F32)
        cot = jnp.concatenate(
            [jnp.where(first, own, other), jnp.where(first, other, own)], axis=0
        )
        gate = pre_ref[0, j, 0].astype(F32) + pre_ref[1, j, 0].astype(F32)
        up = pre_ref[0, j, 1].astype(F32) + pre_ref[1, j, 1].astype(F32)
        s = jax.nn.sigmoid(gate)
        d_gate = (cot * up * s * (1.0 + gate * (1.0 - s))).astype(BF16)
        d_up = (cot * gate * s).astype(BF16)
        d_ref[j, 0] = d_gate
        d_ref[j, 1] = d_up
        dg_ref[:, cols] = d_gate.astype(F32)
        du_ref[:, cols] = d_up.astype(F32)
    parts, width = dp_ref.shape[0], dg_ref.shape[1]
    step = width // parts
    for k in range(parts):
        base = (k * step) // GROUP * GROUP
        span = min(2 * GROUP, width - base)
        shift = k * step - base
        for t, src in enumerate((dg_ref, du_ref)):
            window = src[:, base : base + span]
            if shift:
                window = pltpu.roll(window, span - shift, 1)
            dp_ref[k, :, t * GROUP : (t + 1) * GROUP] = window[:, :GROUP].astype(BF16)


def act_grad_kernel(n_x, where_ref, gs_ref, us_ref, *refs):
    d_refs, (gq_ref, uq_ref, out_ref, acc_ref) = refs[:n_x], refs[n_x:]
    j = pl.program_id(0)
    total = None
    for t, (q_ref, s_ref) in enumerate(((gq_ref, gs_ref), (uq_ref, us_ref))):
        w = dequant(q_ref, s_ref, j * (CHUNK // GROUP))
        rows = jnp.concatenate([r[0, t] for r in d_refs], axis=0)
        part = lax.dot_general(rows, w, (((1,), (1,)), ((), ())), preferred_element_type=F32)
        total = part if total is None else total + part

    @pl.when(j == 0)
    def _():
        acc_ref[...] = total

    @pl.when(j > 0)
    def _():
        acc_ref[...] += total

    @pl.when(j == pl.num_programs(0) - 1)
    def _():
        tok = out_ref.shape[1]
        for k in range(n_x):
            at = lax.rem(where_ref[0] - k + n_x, n_x)
            out_ref[pl.ds(at, 1)] = acc_ref[k * tok : (k + 1) * tok, :].astype(BF16)[None]


def weight_grad_kernel(n_x, where_ref, *refs):
    d_refs, (nat_ref, gate_ref, up_ref) = refs[:n_x], refs[n_x:]
    total = None
    for k in range(n_x):
        at = lax.rem(where_ref[0] - k + n_x, n_x)
        rows = d_refs[k][...]
        rows = rows.reshape(rows.shape[0] * rows.shape[1], rows.shape[2])
        nat = nat_ref[:, pl.ds(at, 1)]
        nat = nat.reshape(rows.shape[0], nat.shape[3])
        part = lax.dot_general(rows, nat, (((0,), (0,)), ((), ())), preferred_element_type=F32)
        total = part if total is None else total + part
    width = gate_ref.shape[0]
    gate_ref[...] = total[:width].astype(BF16)
    up_ref[...] = total[GROUP : GROUP + width].astype(BF16)


def params(mib=48):
    return pltpu.CompilerParams(vmem_limit_bytes=mib * 1024 * 1024)


def ring(n, k):
    return [(i, (i + k) % n) for i in range(n)]


def on_device(
    act_values, activation_scale, token_order, gate_q, gate_scale, up_q, up_scale, cotangent
):
    n_x, n_zh = lax.axis_size("x"), lax.axis_size("zh")
    n_depth = lax.axis_size("y") * lax.axis_size("core")
    n_col = lax.axis_size("zl")
    tok, feat = act_values.shape
    hidden = gate_q.shape[1]
    n_chunks = hidden // CHUNK
    rows = tok // n_x
    slice_width = hidden // n_depth
    where = jnp.stack([lax.axis_index("x"), lax.axis_index("zh")]).astype(jnp.int32)
    smem = pl.BlockSpec(memory_space=pltpu.SMEM)
    vmem = pl.BlockSpec(memory_space=pltpu.VMEM)

    cot_other = lax.ppermute(cotangent, "zh", ring(n_zh, 1))

    q_spec = pl.BlockSpec((feat, CHUNK), lambda j: (0, j))
    pre, natural = pl.pallas_call(
        forward_kernel,
        grid=(n_chunks,),
        in_specs=[
            smem,
            smem,
            pl.BlockSpec((tok, feat), lambda j: (0, 0)),
            pl.BlockSpec((feat // GROUP, tok), lambda j: (0, 0)),
            pl.BlockSpec((1, tok), lambda j: (0, 0)),
            q_spec,
            q_spec,
        ],
        out_specs=[
            pl.BlockSpec((n_x, 1, 2, rows, CHUNK), lambda j: (0, j, 0, 0, 0)),
            pl.BlockSpec((tok, feat), lambda j: (0, 0)),
        ],
        out_shape=[
            jax.ShapeDtypeStruct((n_x, n_chunks, 2, rows, CHUNK), BF16),
            jax.ShapeDtypeStruct((tok, feat), BF16),
        ],
        compiler_params=params(),
        name="forward",
    )(gate_scale, up_scale, act_values, activation_scale.T, token_order, gate_q, up_q)

    nat_all = lax.all_gather(natural, ("y", "core"), axis=0, tiled=False)
    nat_all = nat_all.reshape(n_depth, n_x, rows, feat)

    got = lax.all_to_all(pre, "x", 0, 0, tiled=True)
    part = jnp.sum(got.astype(F32), axis=0).astype(BF16)
    both = lax.all_gather(part, "zh", axis=0, tiled=False)

    d, d_split = pl.pallas_call(
        activation_kernel,
        in_specs=[smem, vmem, vmem, vmem],
        out_specs=[vmem, vmem],
        out_shape=[
            jax.ShapeDtypeStruct((n_chunks, 2, rows, CHUNK), BF16),
            jax.ShapeDtypeStruct((n_depth, rows, 2 * GROUP), BF16),
        ],
        scratch_shapes=[pltpu.VMEM((rows, hidden), F32), pltpu.VMEM((rows, hidden), F32)],
        compiler_params=params(),
        name="activation",
    )(where, both, cotangent, cot_other)

    d_x = [d] + [lax.ppermute(d, "x", ring(n_x, k)) for k in range(1, n_x)]
    d_depth = lax.all_to_all(d_split, ("y", "core"), 0, 0, tiled=True)

    d_spec = pl.BlockSpec((1, 2, rows, CHUNK), lambda j: (j, 0, 0, 0))
    act_part = pl.pallas_call(
        functools.partial(act_grad_kernel, n_x),
        grid=(n_chunks,),
        in_specs=[smem, smem, smem] + [d_spec] * n_x + [q_spec, q_spec],
        out_specs=pl.BlockSpec((n_x, rows, feat), lambda j: (0, 0, 0)),
        out_shape=jax.ShapeDtypeStruct((n_x, rows, feat), BF16),
        scratch_shapes=[pltpu.VMEM((tok, feat), F32)],
        compiler_params=params(),
        name="act_grad",
    )(where, gate_scale, up_scale, *d_x, gate_q, up_q)

    d_w = [d_depth] + [lax.ppermute(d_depth, "x", ring(n_x, k)) for k in range(1, n_x)]
    got_act = lax.all_to_all(act_part.reshape(n_col, tok // n_col, feat), "zl", 0, 0, tiled=True)
    grad_act = jnp.sum(got_act.astype(F32), axis=0).astype(BF16)

    gate_t, up_t = pl.pallas_call(
        functools.partial(weight_grad_kernel, n_x),
        in_specs=[smem] + [vmem] * (n_x + 1),
        out_specs=[vmem, vmem],
        out_shape=[jax.ShapeDtypeStruct((slice_width, feat), BF16)] * 2,
        compiler_params=params(),
        name="weight_grad",
    )(where, *d_w, nat_all)
    return grad_act, gate_t.T, up_t.T


def solution(mesh):
    sizes = mesh.shape
    n_zh, n_core = 2, 2
    fine = Mesh(
        mesh.devices.reshape(
            sizes["depth"] // n_core, n_core, sizes["row"] // n_zh, n_zh, sizes["col"]
        ),
        ("y", "core", "x", "zh", "zl"),
    )
    depth, row, col = ("y", "core"), ("x", "zh"), "zl"
    return jax.shard_map(
        on_device,
        mesh=fine,
        in_specs=(
            P(depth, row),
            P(depth, row),
            P(depth, None),
            P(row, col),
            P(row, col),
            P(row, col),
            P(row, col),
            P(depth + row, col),
        ),
        out_specs=(
            P(depth + (col,), row),
            P(row, (col,) + depth),
            P(row, (col,) + depth),
        ),
        check_vma=False,
    )
```

time: 397 us -> 145 us (0.37)
  the two profiles are of different devices: /device:TPU:2 before, /device:TPU:11 now
where the time goes in v1:
time: 145 us; the launch traced here: 144 us
  starting transfers between devices  69.8 us (48%)
  waiting for transfers between devices  19.3 us (13%)
  blocking collectives  18.2 us (13%)
  between operations  14.1 us (10%)
  Pallas kernels  12.3 us (8%)
  local copies, waits for them, and re-layouts  9.7 us (7%)
    all_to_all x1, starting transfers between devices, on_device(): lax.all_to_all(act_part.reshape(n_col, tok // n_col, feat), 'zl', 0, 0, t...  19.8 us
    ppermute x1, starting transfers between devices, on_device(): cot_other = lax.ppermute(cotangent, 'zh', ring(n_zh, 1))  19.2 us
    all_gather x1, blocking collectives, on_device(): both = lax.all_gather(part, 'zh', axis=0, tiled=False)  18.2 us
    unnamed x26, local copies, waits for them, and re-layouts  9.7 us
    ppermute x3, starting transfers between devices, on_device(): d_x = [d] + [lax.ppermute(d, 'x', ring(n_x, k)) for k in range(1, n_x)]  9.57 us
    ppermute x3, waiting for transfers between devices, on_device(): d_x = [d] + [lax.ppermute(d, 'x', ring(n_x, k)) for k in range(1, n_x)]  9.35 us
    ppermute x3, starting transfers between devices, on_device(): lax.ppermute(d_depth, 'x', ring(n_x, k))  8.62 us
    all_to_all x1, starting transfers between devices, on_device(): d_depth = lax.all_to_all(d_split, ('y', 'core'), 0, 0, tiled=True)  8.24 us
  transfers between devices with their start and end apart: 11, of which 5 were waited for; matrix products, arithmetic and copies ran while one was open for 1% of the time, Pallas kernels for 4%

profile of v1, /device:TPU:11, one launch (start us, length us, event | category | flops | bytes accessed | tf_op | source)
XLA Modules:
  0.0 144.4 jit_solution(9100447723533844510)
XLA Ops:
  7.2 0.0 all-gather.4.cloned.1.call-start
  7.2 0.0 copy-start
  7.2 1.5 %copy-done = bf16[512,1792]{1,0:T(8,128)(2,1)S(1)} copy-done((bf16[512,1792]{1,0:T(8,128)(2,1)S(1)}, bf16[512,1792]{1,0:T(8,128)(2,1)}, u32[]{:S(2)}) %copy-start) | copy-done | bytes 1835032
  8.7 0.0 copy-start.2
  8.7 1.5 %copy-done.2 = bf16[512,1792]{1,0:T(8,128)(2,1)S(1)} copy-done((bf16[512,1792]{1,0:T(8,128)(2,1)S(1)}, bf16[512,1792]{1,0:T(8,128)(2,1)}, u32[]{:S(2)}) %copy-start.2) | copy-done | bytes 1835032
  10.2 0.0 copy-start.5
  10.2 0.9 copy-done.5
  11.1 0.0 copy-start.7
  11.1 0.7 copy-done.7
  11.8 0.0 copy-start.9
  11.8 0.7 copy-done.9
  12.5 0.0 copy-start.11
  12.5 0.7 copy-done.11
  13.2 0.0 copy-start.12
  13.2 0.7 copy-done.12
  13.8 4.8 %forward.1 = (bf16[4,7,2,32,256]{4,3,2,1,0:T(8,128)(2,1)}, bf16[128,512]{1,0:T(8,128)(2,1)}) custom-call(f32[4,14]{1,0:T(4,128)S(1)} %copy-done.7, f32[4,14]{1,0:T(4,128)S(1)} %copy-done.9, bf16[128,512]{1,0:T(8,128)(2,1)S(1)} %copy-done.5, f32[4,128]{1,0:T(4,128)S(1)} %bitcast.10, s32[1,128]{1,0:T(1,128)S(1)} %copy-done.12, bf16[512,1792]{1,0:T(8,128)(2,1)S(1)} %copy-done, ...), custom_call_target="tpu_custom_call" | custom-call | tf_op jit(solution)/shard_map/forward/pallas_call | solution.py:152
  18.7 0.0 copy-start.6
  18.7 0.0 all-gather.4.cloned.1.call-update
  18.7 4.3 %all-to-all-start = ((bf16[4,7,2,32,256]{4,3,2,1,0:T(8,128)(2,1)}), bf16[4,7,2,32,256]{4,3,2,1,0:T(8,128)(2,1)S(1)}, u32[]{:S(2)}, u32[]{:S(2)}) async-start(bf16[4,7,2,32,256]{4,3,2,1,0:T(8,128)(2,1)} %get-tuple-element.9), calls=%async_computation | async-start | bytes 1835008 | tf_op jit(solution)/shard_map/all_to_all | solution.py:179
  23.0 0.0 copy-done.6
  23.0 0.0 copy-start.1
  23.0 0.0 copy-start.8
  23.0 0.0 copy-start.10
  23.0 19.2 %collective-permute-start = (bf16[16,1792]{1,0:T(8,128)(2,1)S(1)}, bf16[16,1792]{1,0:T(8,128)(2,1)S(1)}, u32[]{:S(2)}, u32[]{:S(2)}) collective-permute-start(bf16[16,1792]{1,0:T(8,128)(2,1)S(1)} %copy-done.6), channel_id=1, source_target_pairs={{0,8},{8,0},{1,9},{9,1},{2,10},{10,2},{3,11},{11,3},{4,12},{12,4},... | collective-permute-start | bytes 172040 | tf_op jit(solution)/shard_map/ppermute | solution.py:149
  42.2 0.1 pad_add_fusion.where_ref
  42.3 0.0 all-to-all-done
  42.3 0.2 reduce_sum.24
  42.5 18.2 %all-gather = bf16[14,2,32,256]{3,2,1,0:T(8,128)(2,1)S(1)} all-gather(bf16[7,2,32,256]{3,2,1,0:T(8,128)(2,1)S(1)} %reduce_sum.24), channel_id=2, replica_groups=mesh['y'=8,'core'=2,'x'=4,'zh'=2,'zl'=8] {'zh'}, dimensions={0}, use_global_device_ids=true | all-gather | bytes 688128 | tf_op jit(solution)/shard_map/all_gather | solution.py:181
  60.7 0.0 collective-permute-done.other_ref
  60.7 1.5 %activation.1 = (bf16[7,2,32,256]{3,2,1,0:T(8,128)(2,1)S(1)}, bf16[16,32,256]{2,1,0:T(8,128)(2,1)}) custom-call(s32[2]{0:T(128)S(1)} %pad_add_fusion.where_ref, bf16[2,7,2,32,256]{4,3,2,1,0:T(8,128)(2,1)S(1)} %bitcast.9, bf16[16,1792]{1,0:T(8,128)(2,1)S(1)} %copy-done.6, bf16[16,1792]{1,0:T(8,128)(2,1)S(1)} %collective-permute-done.other_ref), custom_call_target="tpu_custom_call" | custom-call | tf_op jit(solution)/shard_map/activation/pallas_call | solution.py:183
  62.2 8.2 %all-to-all-start.2 = ((bf16[16,32,256]{2,1,0:T(8,128)(2,1)}), bf16[16,32,256]{2,1,0:T(8,128)(2,1)S(1)}, u32[]{:S(2)}, u32[]{:S(2)}) async-start(bf16[16,32,256]{2,1,0:T(8,128)(2,1)} %get-tuple-element.11), calls=%async_computation.2 | async-start | bytes 524288 | tf_op jit(solution)/shard_map/all_to_all | solution.py:197
  70.5 3.1 %collective-permute-start.1 = (bf16[7,2,32,256]{3,2,1,0:T(8,128)(2,1)S(1)}, bf16[7,2,32,256]{3,2,1,0:T(8,128)(2,1)S(1)}, u32[]{:S(2)}, u32[]{:S(2)}) collective-permute-start(bf16[7,2,32,256]{3,2,1,0:T(8,128)(2,1)S(1)} %get-tuple-element.10.refs_0_), channel_id=1, source_target_pairs={{0,16},{16,32},{32,48},{48,0},{1,17},{17,33},{33,49},{49,1},{2,18}... | collective-permute-start | bytes 688136 | tf_op jit(solution)/shard_map/ppermute | solution.py:196
  73.6 2.9 %collective-permute-start.2 = (bf16[7,2,32,256]{3,2,1,0:T(8,128)(2,1)S(1)}, bf16[7,2,32,256]{3,2,1,0:T(8,128)(2,1)S(1)}, u32[]{:S(2)}, u32[]{:S(2)}) collective-permute-start(bf16[7,2,32,256]{3,2,1,0:T(8,128)(2,1)S(1)} %get-tuple-element.10.refs_0_), channel_id=1, source_target_pairs={{0,32},{16,48},{32,0},{48,16},{1,33},{17,49},{33,1},{49,17},{2,34}... | collective-permute-start | bytes 688136 | tf_op jit(solution)/shard_map/ppermute | solution.py:196
  76.5 3.6 %collective-permute-start.3 = (bf16[7,2,32,256]{3,2,1,0:T(8,128)(2,1)S(1)}, bf16[7,2,32,256]{3,2,1,0:T(8,128)(2,1)S(1)}, u32[]{:S(2)}, u32[]{:S(2)}) collective-permute-start(bf16[7,2,32,256]{3,2,1,0:T(8,128)(2,1)S(1)} %get-tuple-element.10.refs_0_), channel_id=1, source_target_pairs={{0,48},{16,0},{32,16},{48,32},{1,49},{17,1},{33,17},{49,33},{2,50}... | collective-permute-start | bytes 688136 | tf_op jit(solution)/shard_map/ppermute | solution.py:196
  80.1 0.0 collective-permute-done.1.refs_1_
  80.1 3.5 %collective-permute-done.2.refs_2_ = bf16[7,2,32,256]{3,2,1,0:T(8,128)(2,1)S(1)} collective-permute-done((bf16[7,2,32,256]{3,2,1,0:T(8,128)(2,1)S(1)}, bf16[7,2,32,256]{3,2,1,0:T(8,128)(2,1)S(1)}, u32[]{:S(2)}, u32[]{:S(2)}) %collective-permute-start.2) | collective-permute-done | bytes 229408 | tf_op jit(solution)/shard_map/ppermute | solution.py:196
  83.5 5.9 %collective-permute-done.3.refs_3_ = bf16[7,2,32,256]{3,2,1,0:T(8,128)(2,1)S(1)} collective-permute-done((bf16[7,2,32,256]{3,2,1,0:T(8,128)(2,1)S(1)}, bf16[7,2,32,256]{3,2,1,0:T(8,128)(2,1)S(1)}, u32[]{:S(2)}, u32[]{:S(2)}) %collective-permute-start.3) | collective-permute-done | bytes 229408 | tf_op jit(solution)/shard_map/ppermute | solution.py:196
  89.4 0.0 copy-done.1
  89.4 0.0 copy-done.8
  89.4 0.0 copy-done.10
  89.4 0.0 copy-start.3
  89.5 1.5 %copy-done.3 = bf16[512,1792]{1,0:T(8,128)(2,1)S(1)} copy-done((bf16[512,1792]{1,0:T(8,128)(2,1)S(1)}, bf16[512,1792]{1,0:T(8,128)(2,1)}, u32[]{:S(2)}) %copy-start.3) | copy-done | bytes 1835032
  90.9 4.0 %act_grad.1 = bf16[4,32,512]{2,1,0:T(8,128)(2,1)} custom-call(s32[2]{0:T(128)S(1)} %pad_add_fusion.where_ref, f32[4,14]{1,0:T(4,128)S(1)} %copy-done.8, f32[4,14]{1,0:T(4,128)S(1)} %copy-done.10, bf16[7,2,32,256]{3,2,1,0:T(8,128)(2,1)S(1)} %get-tuple-element.10.refs_0_, bf16[7,2,32,256]{3,2,1,0:T(8,128)(2,1)S(1)} %collective-permute-done.1.refs_1_, ...), custom_call_target="tpu_custom_call" | custom-call | tf_op jit(solution)/shard_map/act_grad/pallas_call | solution.py:200
  95.0 0.0 all-to-all-done.2.refs_0_
  95.0 19.8 %all-to-all-start.1 = ((bf16[8,16,512]{2,1,0:T(8,128)(2,1)}), bf16[8,16,512]{2,1,0:T(8,128)(2,1)S(1)}, u32[]{:S(2)}, u32[]{:S(2)}) async-start(bf16[8,16,512]{2,1,0:T(8,128)(2,1)} %bitcast.4), calls=%async_computation.1 | async-start | bytes 262144 | tf_op jit(solution)/shard_map/all_to_all | solution.py:212
  114.8 1.9 %collective-permute-start.4 = (bf16[16,32,256]{2,1,0:T(8,128)(2,1)S(1)}, bf16[16,32,256]{2,1,0:T(8,128)(2,1)S(1)}, u32[]{:S(2)}, u32[]{:S(2)}) collective-permute-start(bf16[16,32,256]{2,1,0:T(8,128)(2,1)S(1)} %all-to-all-done.2.refs_0_), channel_id=1, source_target_pairs={{0,16},{16,32},{32,48},{48,0},{1,17},{17,33},{33,49},{49,1},{2,18}... | collective-permute-start | bytes 786440 | tf_op jit(solution)/shard_map/ppermute | solution.py:211
  116.7 2.7 %collective-permute-start.5 = (bf16[16,32,256]{2,1,0:T(8,128)(2,1)S(1)}, bf16[16,32,256]{2,1,0:T(8,128)(2,1)S(1)}, u32[]{:S(2)}, u32[]{:S(2)}) collective-permute-start(bf16[16,32,256]{2,1,0:T(8,128)(2,1)S(1)} %all-to-all-done.2.refs_0_), channel_id=1, source_target_pairs={{0,32},{16,48},{32,0},{48,16},{1,33},{17,49},{33,1},{49,17},{2,34}... | collective-permute-start | bytes 786440 | tf_op jit(solution)/shard_map/ppermute | solution.py:211
  119.5 4.0 %collective-permute-start.6 = (bf16[16,32,256]{2,1,0:T(8,128)(2,1)S(1)}, bf16[16,32,256]{2,1,0:T(8,128)(2,1)S(1)}, u32[]{:S(2)}, u32[]{:S(2)}) collective-permute-start(bf16[16,32,256]{2,1,0:T(8,128)(2,1)S(1)} %all-to-all-done.2.refs_0_), channel_id=1, source_target_pairs={{0,48},{16,0},{32,16},{48,32},{1,49},{17,1},{33,17},{49,33},{2,50}... | collective-permute-start | bytes 786440 | tf_op jit(solution)/shard_map/ppermute | solution.py:211
  123.5 1.7 %all-to-all-done.1 = bf16[8,16,512]{2,1,0:T(8,128)(2,1)S(1)} async-done(((bf16[8,16,512]{2,1,0:T(8,128)(2,1)}), bf16[8,16,512]{2,1,0:T(8,128)(2,1)S(1)}, u32[]{:S(2)}, u32[]{:S(2)}) %all-to-all-start.1) | async-done | bytes 131104 | tf_op jit(solution)/shard_map/all_to_all | solution.py:212
  125.2 0.6 reduce_sum.25
  125.8 0.0 collective-permute-done.4.refs_1_
  125.8 0.8 collective-permute-done.5.refs_2_
  126.6 7.4 %collective-permute-done.6.refs_3_ = bf16[16,32,256]{2,1,0:T(8,128)(2,1)S(1)} collective-permute-done((bf16[16,32,256]{2,1,0:T(8,128)(2,1)S(1)}, bf16[16,32,256]{2,1,0:T(8,128)(2,1)S(1)}, u32[]{:S(2)}, u32[]{:S(2)}) %collective-permute-start.6) | collective-permute-done | bytes 262176 | tf_op jit(solution)/shard_map/ppermute | solution.py:211
  134.0 0.0 all-gather.4.cloned.1.call-done
  134.0 0.0 copy-start.4
  134.0 1.6 %copy-done.4 = bf16[2048,512]{1,0:T(8,128)(2,1)S(1)} copy-done((bf16[2048,512]{1,0:T(8,128)(2,1)S(1)}, bf16[2048,512]{1,0:T(8,128)(2,1)}, u32[]{:S(2)}) %copy-start.4) | copy-done | bytes 2097176
  135.6 1.9 %weight_grad.1 = (bf16[112,512]{1,0:T(8,128)(2,1)}, bf16[112,512]{1,0:T(8,128)(2,1)}) custom-call(s32[2]{0:T(128)S(1)} %pad_add_fusion.where_ref, bf16[16,32,256]{2,1,0:T(8,128)(2,1)S(1)} %all-to-all-done.2.refs_0_, bf16[16,32,256]{2,1,0:T(8,128)(2,1)S(1)} %collective-permute-done.4.refs_1_, bf16[16,32,256]{2,1,0:T(8,128)(2,1)S(1)} %collective-permute-done.5.refs_2_, ...), custom_call_target="tpu_custom_call" | custom-call | tf_op jit(solution)/shard_map/weight_grad/pallas_call | solution.py:215
Async XLA Ops:
  7.2 126.8 %all-gather.4.cloned.1.call-start = ((), (), s32[]{:S(2)}) async-start(), calls=%async_computation.3 | async-start | bytes 2228224 | tf_op jit(solution)/shard_map/all_gather | solution.py:176
  7.2 1.5 %copy-start = (bf16[512,1792]{1,0:T(8,128)(2,1)S(1)}, bf16[512,1792]{1,0:T(8,128)(2,1)}, u32[]{:S(2)}) copy-start(bf16[512,1792]{1,0:T(8,128)(2,1)} %refs_4_.1) | copy-start | bytes 5505028
  8.7 1.5 %copy-start.2 = (bf16[512,1792]{1,0:T(8,128)(2,1)S(1)}, bf16[512,1792]{1,0:T(8,128)(2,1)}, u32[]{:S(2)}) copy-start(bf16[512,1792]{1,0:T(8,128)(2,1)} %refs_5_.1) | copy-start | bytes 5505028
  10.2 0.9 copy-start.5
  11.1 0.7 copy-start.7
  11.8 0.7 copy-start.9
  12.5 0.7 copy-start.11
  13.2 0.7 copy-start.12
  18.7 4.3 %copy-start.6 = (bf16[16,1792]{1,0:T(8,128)(2,1)S(1)}, bf16[16,1792]{1,0:T(8,128)(2,1)}, u32[]{:S(2)}) copy-start(bf16[16,1792]{1,0:T(8,128)(2,1)} %own_ref.1) | copy-start | bytes 172036
  18.7 23.6 %all-to-all-start = ((bf16[4,7,2,32,256]{4,3,2,1,0:T(8,128)(2,1)}), bf16[4,7,2,32,256]{4,3,2,1,0:T(8,128)(2,1)S(1)}, u32[]{:S(2)}, u32[]{:S(2)}) async-start(bf16[4,7,2,32,256]{4,3,2,1,0:T(8,128)(2,1)} %get-tuple-element.9), calls=%async_computation | async-start | bytes 1835008 | tf_op jit(solution)/shard_map/all_to_all | solution.py:179
  23.0 66.5 %copy-start.1 = (bf16[512,1792]{1,0:T(8,128)(2,1)S(1)}, bf16[512,1792]{1,0:T(8,128)(2,1)}, u32[]{:S(2)}) copy-start(bf16[512,1792]{1,0:T(8,128)(2,1)} %refs_4_.1) | copy-start | bytes 5505028
  23.0 66.5 %copy-start.8 = (f32[4,14]{1,0:T(4,128)S(1)}, f32[4,14]{1,0:T(4,128)}, u32[]{:S(2)}) copy-start(f32[4,14]{1,0:T(4,128)} %gs_ref.3) | copy-start | bytes 676
  23.0 66.5 %copy-start.10 = (f32[4,14]{1,0:T(4,128)S(1)}, f32[4,14]{1,0:T(4,128)}, u32[]{:S(2)}) copy-start(f32[4,14]{1,0:T(4,128)} %us_ref.3) | copy-start | bytes 676
  23.0 37.7 %collective-permute-start = (bf16[16,1792]{1,0:T(8,128)(2,1)S(1)}, bf16[16,1792]{1,0:T(8,128)(2,1)S(1)}, u32[]{:S(2)}, u32[]{:S(2)}) collective-permute-start(bf16[16,1792]{1,0:T(8,128)(2,1)S(1)} %copy-done.6), channel_id=1, source_target_pairs={{0,8},{8,0},{1,9},{9,1},{2,10},{10,2},{3,11},{11,3},{4,12},{12,4},... | collective-permute-start | bytes 172040 | tf_op jit(solution)/shard_map/ppermute | solution.py:149
  62.2 32.8 %all-to-all-start.2 = ((bf16[16,32,256]{2,1,0:T(8,128)(2,1)}), bf16[16,32,256]{2,1,0:T(8,128)(2,1)S(1)}, u32[]{:S(2)}, u32[]{:S(2)}) async-start(bf16[16,32,256]{2,1,0:T(8,128)(2,1)} %get-tuple-element.11), calls=%async_computation.2 | async-start | bytes 524288 | tf_op jit(solution)/shard_map/all_to_all | solution.py:197
  70.5 9.6 %collective-permute-start.1 = (bf16[7,2,32,256]{3,2,1,0:T(8,128)(2,1)S(1)}, bf16[7,2,32,256]{3,2,1,0:T(8,128)(2,1)S(1)}, u32[]{:S(2)}, u32[]{:S(2)}) collective-permute-start(bf16[7,2,32,256]{3,2,1,0:T(8,128)(2,1)S(1)} %get-tuple-element.10.refs_0_), channel_id=1, source_target_pairs={{0,16},{16,32},{32,48},{48,0},{1,17},{17,33},{33,49},{49,1},{2,18}... | collective-permute-start | bytes 688136 | tf_op jit(solution)/shard_map/ppermute | solution.py:196
  73.6 10.0 %collective-permute-start.2 = (bf16[7,2,32,256]{3,2,1,0:T(8,128)(2,1)S(1)}, bf16[7,2,32,256]{3,2,1,0:T(8,128)(2,1)S(1)}, u32[]{:S(2)}, u32[]{:S(2)}) collective-permute-start(bf16[7,2,32,256]{3,2,1,0:T(8,128)(2,1)S(1)} %get-tuple-element.10.refs_0_), channel_id=1, source_target_pairs={{0,32},{16,48},{32,0},{48,16},{1,33},{17,49},{33,1},{49,17},{2,34}... | collective-permute-start | bytes 688136 | tf_op jit(solution)/shard_map/ppermute | solution.py:196
  76.5 13.0 %collective-permute-start.3 = (bf16[7,2,32,256]{3,2,1,0:T(8,128)(2,1)S(1)}, bf16[7,2,32,256]{3,2,1,0:T(8,128)(2,1)S(1)}, u32[]{:S(2)}, u32[]{:S(2)}) collective-permute-start(bf16[7,2,32,256]{3,2,1,0:T(8,128)(2,1)S(1)} %get-tuple-element.10.refs_0_), channel_id=1, source_target_pairs={{0,48},{16,0},{32,16},{48,32},{1,49},{17,1},{33,17},{49,33},{2,50}... | collective-permute-start | bytes 688136 | tf_op jit(solution)/shard_map/ppermute | solution.py:196
  89.4 1.5 %copy-start.3 = (bf16[512,1792]{1,0:T(8,128)(2,1)S(1)}, bf16[512,1792]{1,0:T(8,128)(2,1)}, u32[]{:S(2)}) copy-start(bf16[512,1792]{1,0:T(8,128)(2,1)} %refs_5_.1) | copy-start | bytes 5505028
  95.0 30.2 %all-to-all-start.1 = ((bf16[8,16,512]{2,1,0:T(8,128)(2,1)}), bf16[8,16,512]{2,1,0:T(8,128)(2,1)S(1)}, u32[]{:S(2)}, u32[]{:S(2)}) async-start(bf16[8,16,512]{2,1,0:T(8,128)(2,1)} %bitcast.4), calls=%async_computation.1 | async-start | bytes 262144 | tf_op jit(solution)/shard_map/all_to_all | solution.py:212
  114.8 11.0 %collective-permute-start.4 = (bf16[16,32,256]{2,1,0:T(8,128)(2,1)S(1)}, bf16[16,32,256]{2,1,0:T(8,128)(2,1)S(1)}, u32[]{:S(2)}, u32[]{:S(2)}) collective-permute-start(bf16[16,32,256]{2,1,0:T(8,128)(2,1)S(1)} %all-to-all-done.2.refs_0_), channel_id=1, source_target_pairs={{0,16},{16,32},{32,48},{48,0},{1,17},{17,33},{33,49},{49,1},{2,18}... | collective-permute-start | bytes 786440 | tf_op jit(solution)/shard_map/ppermute | solution.py:211
  116.7 9.9 %collective-permute-start.5 = (bf16[16,32,256]{2,1,0:T(8,128)(2,1)S(1)}, bf16[16,32,256]{2,1,0:T(8,128)(2,1)S(1)}, u32[]{:S(2)}, u32[]{:S(2)}) collective-permute-start(bf16[16,32,256]{2,1,0:T(8,128)(2,1)S(1)} %all-to-all-done.2.refs_0_), channel_id=1, source_target_pairs={{0,32},{16,48},{32,0},{48,16},{1,33},{17,49},{33,1},{49,17},{2,34}... | collective-permute-start | bytes 786440 | tf_op jit(solution)/shard_map/ppermute | solution.py:211
  119.5 14.5 %collective-permute-start.6 = (bf16[16,32,256]{2,1,0:T(8,128)(2,1)S(1)}, bf16[16,32,256]{2,1,0:T(8,128)(2,1)S(1)}, u32[]{:S(2)}, u32[]{:S(2)}) collective-permute-start(bf16[16,32,256]{2,1,0:T(8,128)(2,1)S(1)} %all-to-all-done.2.refs_0_), channel_id=1, source_target_pairs={{0,48},{16,0},{32,16},{48,32},{1,49},{17,1},{33,17},{49,33},{2,50}... | collective-permute-start | bytes 786440 | tf_op jit(solution)/shard_map/ppermute | solution.py:211
  134.0 1.6 %copy-start.4 = (bf16[2048,512]{1,0:T(8,128)(2,1)S(1)}, bf16[2048,512]{1,0:T(8,128)(2,1)}, u32[]{:S(2)}) copy-start(bf16[2048,512]{1,0:T(8,128)(2,1)} %all-gather.4.cloned.1.call-done) | copy-start | bytes 6291460
Sparse Core Ops, SparseCore 0:
  18.8 54.9 all-gather.3

commit v2 on v1

--- a/solution.py
+++ b/solution.py
@@ -1,5 +1,3 @@
-import functools
-
 import jax
 import jax.numpy as jnp
 from jax import lax
@@ -50,17 +48,27 @@
         pre_ref[:, 0, t] = out.reshape(pre_ref.shape[0], pre_ref.shape[3], CHUNK)
 
 
-def activation_kernel(where_ref, pre_ref, own_ref, other_ref, d_ref, dp_ref, dg_ref, du_ref):
-    first = where_ref[1] == 0
-    n_chunks = pre_ref.shape[1]
+def reduce_kernel(got_ref, cot_ref, out_ref):
+    n_chunks, rows = got_ref.shape[1], got_ref.shape[3]
+    for j in range(n_chunks):
+        for t in range(2):
+            total = got_ref[0, j, t].astype(F32)
+            for i in range(1, got_ref.shape[0]):
+                total += got_ref[i, j, t].astype(F32)
+            out_ref[j, t * rows : (t + 1) * rows] = total.astype(BF16)
+        out_ref[j, 2 * rows :] = cot_ref[:, j * CHUNK : (j + 1) * CHUNK]
+
+
+def activation_kernel(pre_ref, d_ref, dp_ref, dg_ref, du_ref):
+    n_zh, n_chunks = pre_ref.shape[0], pre_ref.shape[1]
+    rows = dp_ref.shape[1]
     for j in range(n_chunks):
         cols = slice(j * CHUNK, (j + 1) * CHUNK)
-        own, other = own_ref[:, cols].astype(F32), other_ref[:, cols].astype(F32)
-        cot = jnp.concatenate(
-            [jnp.where(first, own, other), jnp.where(first, other, own)], axis=0
+        gate, up = (
+            sum(pre_ref[i, j, t * rows : (t + 1) * rows].astype(F32) for i in range(n_zh))
+            for t in range(2)
         )
-        gate = pre_ref[0, j, 0].astype(F32) + pre_ref[1, j, 0].astype(F32)
-        up = pre_ref[0, j, 1].astype(F32) + pre_ref[1, j, 1].astype(F32)
+        cot = jnp.concatenate([pre_ref[i, j, 2 * rows :] for i in range(n_zh)], axis=0).astype(F32)
         s = jax.nn.sigmoid(gate)
         d_gate = (cot * up * s * (1.0 + gate * (1.0 - s))).astype(BF16)
         d_up = (cot * gate * s).astype(BF16)
@@ -81,13 +89,12 @@
             dp_ref[k, :, t * GROUP : (t + 1) * GROUP] = window[:, :GROUP].astype(BF16)
 
 
-def act_grad_kernel(n_x, where_ref, gs_ref, us_ref, *refs):
-    d_refs, (gq_ref, uq_ref, out_ref, acc_ref) = refs[:n_x], refs[n_x:]
+def act_grad_kernel(gs_ref, us_ref, d_ref, gq_ref, uq_ref, out_ref, acc_ref):
     j = pl.program_id(0)
     total = None
     for t, (q_ref, s_ref) in enumerate(((gq_ref, gs_ref), (uq_ref, us_ref))):
         w = dequant(q_ref, s_ref, j * (CHUNK // GROUP))
-        rows = jnp.concatenate([r[0, t] for r in d_refs], axis=0)
+        rows = d_ref[:, 0, t].reshape(acc_ref.shape[0], CHUNK)
         part = lax.dot_general(rows, w, (((1,), (1,)), ((), ())), preferred_element_type=F32)
         total = part if total is None else total + part
 
@@ -101,34 +108,33 @@
 
     @pl.when(j == pl.num_programs(0) - 1)
     def _():
-        tok = out_ref.shape[1]
-        for k in range(n_x):
-            at = lax.rem(where_ref[0] - k + n_x, n_x)
-            out_ref[pl.ds(at, 1)] = acc_ref[k * tok : (k + 1) * tok, :].astype(BF16)[None]
-
-
-def weight_grad_kernel(n_x, where_ref, *refs):
-    d_refs, (nat_ref, gate_ref, up_ref) = refs[:n_x], refs[n_x:]
-    total = None
-    for k in range(n_x):
-        at = lax.rem(where_ref[0] - k + n_x, n_x)
-        rows = d_refs[k][...]
-        rows = rows.reshape(rows.shape[0] * rows.shape[1], rows.shape[2])
-        nat = nat_ref[:, pl.ds(at, 1)]
-        nat = nat.reshape(rows.shape[0], nat.shape[3])
-        part = lax.dot_general(rows, nat, (((0,), (0,)), ((), ())), preferred_element_type=F32)
-        total = part if total is None else total + part
-    width = gate_ref.shape[0]
-    gate_ref[...] = total[:width].astype(BF16)
-    up_ref[...] = total[GROUP : GROUP + width].astype(BF16)
-
-
-def params(mib=48):
+        out_ref[...] = acc_ref[...].astype(BF16)
+
+
+def finish_kernel(dw_ref, nat_ref, got_ref, gate_ref, up_ref, act_ref, acc_ref):
+    k = pl.program_id(0)
+    rows = dw_ref[0].reshape(dw_ref.shape[1] * dw_ref.shape[2], dw_ref.shape[3])
+    nat = nat_ref[:, 0].reshape(rows.shape[0], nat_ref.shape[3])
+    part = lax.dot_general(rows, nat, (((0,), (0,)), ((), ())), preferred_element_type=F32)
+
+    @pl.when(k == 0)
+    def _():
+        acc_ref[...] = part
+        act_ref[...] = sum(got_ref[i].astype(F32) for i in range(got_ref.shape[0])).astype(BF16)
+
+    @pl.when(k > 0)
+    def _():
+        acc_ref[...] += part
+
+    @pl.when(k == pl.num_programs(0) - 1)
+    def _():
+        width = gate_ref.shape[0]
+        gate_ref[...] = acc_ref[:width].astype(BF16)
+        up_ref[...] = acc_ref[GROUP : GROUP + width].astype(BF16)
+
+
+def params(mib=60):
     return pltpu.CompilerParams(vmem_limit_bytes=mib * 1024 * 1024)
-
-
-def ring(n, k):
-    return [(i, (i + k) % n) for i in range(n)]
 
 
 def on_device(
@@ -142,11 +148,8 @@
     n_chunks = hidden // CHUNK
     rows = tok // n_x
     slice_width = hidden // n_depth
-    where = jnp.stack([lax.axis_index("x"), lax.axis_index("zh")]).astype(jnp.int32)
     smem = pl.BlockSpec(memory_space=pltpu.SMEM)
     vmem = pl.BlockSpec(memory_space=pltpu.VMEM)
-
-    cot_other = lax.ppermute(cotangent, "zh", ring(n_zh, 1))
 
     q_spec = pl.BlockSpec((feat, CHUNK), lambda j: (0, j))
     pre, natural = pl.pallas_call(
@@ -177,49 +180,76 @@
     nat_all = nat_all.reshape(n_depth, n_x, rows, feat)
 
     got = lax.all_to_all(pre, "x", 0, 0, tiled=True)
-    part = jnp.sum(got.astype(F32), axis=0).astype(BF16)
-    both = lax.all_gather(part, "zh", axis=0, tiled=False)
+    packed = pl.pallas_call(
+        reduce_kernel,
+        in_specs=[vmem, vmem],
+        out_specs=vmem,
+        out_shape=jax.ShapeDtypeStruct((n_chunks, 2 * rows + rows // n_zh, CHUNK), BF16),
+        compiler_params=params(16),
+        name="reduce",
+    )(got, cotangent)
+    both = lax.all_gather(packed, "zh", axis=0, tiled=False)
 
     d, d_split = pl.pallas_call(
         activation_kernel,
-        in_specs=[smem, vmem, vmem, vmem],
+        in_specs=[vmem],
         out_specs=[vmem, vmem],
         out_shape=[
             jax.ShapeDtypeStruct((n_chunks, 2, rows, CHUNK), BF16),
             jax.ShapeDtypeStruct((n_depth, rows, 2 * GROUP), BF16),
         ],
         scratch_shapes=[pltpu.VMEM((rows, hidden), F32), pltpu.VMEM((rows, hidden), F32)],
-        compiler_params=params(),
+        compiler_params=params(16),
         name="activation",
-    )(where, both, cotangent, cot_other)
-
-    d_x = [d] + [lax.ppermute(d, "x", ring(n_x, k)) for k in range(1, n_x)]
+    )(both)
+
     d_depth = lax.all_to_all(d_split, ("y", "core"), 0, 0, tiled=True)
-
-    d_spec = pl.BlockSpec((1, 2, rows, CHUNK), lambda j: (j, 0, 0, 0))
+    d_all = lax.all_gather(d, "x", axis=0, tiled=False)
+    d_all, d_depth = lax.optimization_barrier((d_all, d_depth))
+    d_copies = jnp.broadcast_to(d_depth[None], (n_x,) + d_depth.shape)
+    d_w = lax.all_to_all(d_copies, "x", 0, 0, tiled=True)
+
     act_part = pl.pallas_call(
-        functools.partial(act_grad_kernel, n_x),
+        act_grad_kernel,
         grid=(n_chunks,),
-        in_specs=[smem, smem, smem] + [d_spec] * n_x + [q_spec, q_spec],
-        out_specs=pl.BlockSpec((n_x, rows, feat), lambda j: (0, 0, 0)),
-        out_shape=jax.ShapeDtypeStruct((n_x, rows, feat), BF16),
+        in_specs=[
+            smem,
+            smem,
+            pl.BlockSpec((n_x, 1, 2, rows, CHUNK), lambda j: (0, j, 0, 0, 0)),
+            q_spec,
+            q_spec,
+        ],
+        out_specs=pl.BlockSpec((tok, feat), lambda j: (0, 0)),
+        out_shape=jax.ShapeDtypeStruct((tok, feat), BF16),
         scratch_shapes=[pltpu.VMEM((tok, feat), F32)],
         compiler_params=params(),
         name="act_grad",
-    )(where, gate_scale, up_scale, *d_x, gate_q, up_q)
-
-    d_w = [d_depth] + [lax.ppermute(d_depth, "x", ring(n_x, k)) for k in range(1, n_x)]
+    )(gate_scale, up_scale, d_all, gate_q, up_q)
+
+    act_part, d_w = lax.optimization_barrier((act_part, d_w))
     got_act = lax.all_to_all(act_part.reshape(n_col, tok // n_col, feat), "zl", 0, 0, tiled=True)
-    grad_act = jnp.sum(got_act.astype(F32), axis=0).astype(BF16)
-
-    gate_t, up_t = pl.pallas_call(
-        functools.partial(weight_grad_kernel, n_x),
-        in_specs=[smem] + [vmem] * (n_x + 1),
-        out_specs=[vmem, vmem],
-        out_shape=[jax.ShapeDtypeStruct((slice_width, feat), BF16)] * 2,
+    gate_t, up_t, grad_act = pl.pallas_call(
+        finish_kernel,
+        grid=(n_x,),
+        in_specs=[
+            pl.BlockSpec((1, n_depth, rows, 2 * GROUP), lambda k: (k, 0, 0, 0)),
+            pl.BlockSpec((n_depth, 1, rows, feat), lambda k: (0, k, 0, 0)),
+            pl.BlockSpec((n_col, tok // n_col, feat), lambda k: (0, 0, 0)),
+        ],
+        out_specs=[
+            pl.BlockSpec((slice_width, feat), lambda k: (0, 0)),
+            pl.BlockSpec((slice_width, feat), lambda k: (0, 0)),
+            pl.BlockSpec((tok // n_col, feat), lambda k: (0, 0)),
+        ],
+        out_shape=[
+            jax.ShapeDtypeStruct((slice_width, feat), BF16),
+            jax.ShapeDtypeStruct((slice_width, feat), BF16),
+            jax.ShapeDtypeStruct((tok // n_col, feat), BF16),
+        ],
+        scratch_shapes=[pltpu.VMEM((2 * GROUP, feat), F32)],
         compiler_params=params(),
-        name="weight_grad",
-    )(where, *d_w, nat_all)
+        name="finish",
+    )(d_w, nat_all, got_act)
     return grad_act, gate_t.T, up_t.T
 
 

time: 145 us -> 146 us (level)
  the two profiles are of different devices: /device:TPU:11 before, /device:TPU:2 now
where the time goes in v2:
time: 146 us; the launch traced here: 145 us
  blocking collectives  93.3 us (64%)
  Pallas kernels  18.4 us (13%)
  between operations  14.1 us (10%)
  starting transfers between devices  12.6 us (9%)
  waiting for transfers between devices  5.74 us (4%)
    all_to_all x1, blocking collectives, on_device(): lax.all_to_all(act_part.reshape(n_col, tok // n_col, feat), 'zl', 0, 0, t...  37.2 us
    all_to_all x1, blocking collectives, on_device(): got = lax.all_to_all(pre, 'x', 0, 0, tiled=True)  25.4 us
    all_gather x1, blocking collectives, on_device(): both = lax.all_gather(packed, 'zh', axis=0, tiled=False)  16.3 us
    all_gather x1, blocking collectives, on_device(): d_all = lax.all_gather(d, 'x', axis=0, tiled=False)  14.4 us
    all_to_all x1, starting transfers between devices, on_device(): d_depth = lax.all_to_all(d_split, ('y', 'core'), 0, 0, tiled=True)  6.6 us
    pallas_call x1, Pallas kernels, on_device(): pl.pallas_call(forward_kernel, grid=(n_chunks,), in_specs=[smem, smem, pl...  6.59 us
    pallas_call x1, Pallas kernels, on_device(): pl.pallas_call(act_grad_kernel, grid=(n_chunks,), in_specs=[smem, smem, p...  6.53 us
    all_to_all x1, starting transfers between devices, on_device(): d_w = lax.all_to_all(d_copies, 'x', 0, 0, tiled=True)  5.94 us
  transfers between devices with their start and end apart: 3, of which 1 were waited for; matrix products, arithmetic and copies ran while one was open for 1% of the time, Pallas kernels for 5%

profile of v2, /device:TPU:2, one launch (start us, length us, event | category | flops | bytes accessed | tf_op | source)
XLA Modules:
  0.0 145.2 jit_solution(11953233901110825738)
XLA Ops:
  7.2 0.0 all-gather.5.cloned.1.call-start
  7.2 6.6 %forward.1 = (bf16[4,7,2,32,256]{4,3,2,1,0:T(8,128)(2,1)}, bf16[128,512]{1,0:T(8,128)(2,1)}) custom-call(f32[4,14]{1,0:T(4,128)} %gs_ref.3, f32[4,14]{1,0:T(4,128)} %us_ref.3, bf16[128,512]{1,0:T(8,128)(2,1)} %act_ref.1, f32[4,128]{1,0:T(4,128)} %bitcast.11, s32[1,128]{1,0:T(1,128)} %order_ref.1, bf16[512,1792]{1,0:T(8,128)(2,1)} %gq_ref.3, ...), custom_call_target="tpu_custom_call" | custom-call | tf_op jit(solution)/shard_map/forward/pallas_call | solution.py:155
  13.8 0.0 copy-start
  13.8 0.0 all-gather.5.cloned.1.call-update
  13.8 25.4 %all_to_all.20.got_ref = bf16[4,7,2,32,256]{4,3,2,1,0:T(8,128)(2,1)S(1)} all-to-all(bf16[4,7,2,32,256]{4,3,2,1,0:T(8,128)(2,1)} %get-tuple-element.14), channel_id=1, replica_groups=mesh['y'=8,'core'=2,'x'=4,'zh'=2,'zl'=8] {'x'}, dimensions={0} | all-to-all | bytes 1835008 | tf_op jit(solution)/shard_map/all_to_all | solution.py:182
  39.2 0.0 copy-done
  39.2 0.1 reduce.1
  39.4 16.3 %all-gather = bf16[14,80,256]{2,1,0:T(8,128)(2,1)S(1)} all-gather(bf16[7,80,256]{2,1,0:T(8,128)(2,1)S(1)} %reduce.1), channel_id=2, replica_groups=mesh['y'=8,'core'=2,'x'=4,'zh'=2,'zl'=8] {'zh'}, dimensions={0}, use_global_device_ids=true | all-gather | bytes 860160 | tf_op jit(solution)/shard_map/all_gather | solution.py:191
  55.7 1.0 activation.1
  56.6 6.6 %all-to-all-start.1 = ((bf16[16,32,256]{2,1,0:T(8,128)(2,1)}), bf16[16,32,256]{2,1,0:T(8,128)(2,1)S(1)}, u32[]{:S(2)}, u32[]{:S(2)}) async-start(bf16[16,32,256]{2,1,0:T(8,128)(2,1)} %get-tuple-element.16), calls=%async_computation.1 | async-start | bytes 524288 | tf_op jit(solution)/shard_map/all_to_all | solution.py:206
  63.2 14.4 %all-gather.1 = bf16[28,2,32,256]{3,2,1,0:T(8,128)(2,1)} all-gather(bf16[7,2,32,256]{3,2,1,0:T(8,128)(2,1)S(1)} %get-tuple-element.15), channel_id=3, replica_groups=mesh['y'=8,'core'=2,'x'=4,'zh'=2,'zl'=8] {'x'}, dimensions={0}, use_global_device_ids=true | all-gather | bytes 1146880 | tf_op jit(solution)/shard_map/all_gather | solution.py:207
  77.6 0.0 all-to-all-done.1
  77.6 1.1 broadcast_in_dim.2
  78.8 5.9 %all-to-all-start.2 = ((bf16[4,16,32,256]{3,2,1,0:T(8,128)(2,1)}), bf16[4,16,32,256]{3,2,1,0:T(8,128)(2,1)S(1)}, u32[]{:S(2)}, u32[]{:S(2)}) async-start(bf16[4,16,32,256]{3,2,1,0:T(8,128)(2,1)} %broadcast_in_dim.2), calls=%async_computation.2 | async-start | bytes 2097152 | tf_op jit(solution)/shard_map/all_to_all | solution.py:210
  84.7 6.5 %act_grad.1 = bf16[128,512]{1,0:T(8,128)(2,1)} custom-call(f32[4,14]{1,0:T(4,128)} %gs_ref.3, f32[4,14]{1,0:T(4,128)} %us_ref.3, bf16[4,7,2,32,256]{4,3,2,1,0:T(8,128)(2,1)} %bitcast.8, bf16[512,1792]{1,0:T(8,128)(2,1)} %gq_ref.3, bf16[512,1792]{1,0:T(8,128)(2,1)} %uq_ref.3), custom_call_target="tpu_custom_call" | custom-call | tf_op jit(solution)/shard_map/act_grad/pallas_call | solution.py:212
  91.2 5.7 %all-to-all-done.2.dw_ref = bf16[4,16,32,256]{3,2,1,0:T(8,128)(2,1)S(1)} async-done(((bf16[4,16,32,256]{3,2,1,0:T(8,128)(2,1)}), bf16[4,16,32,256]{3,2,1,0:T(8,128)(2,1)S(1)}, u32[]{:S(2)}, u32[]{:S(2)}) %all-to-all-start.2) | async-done | bytes 1048608 | tf_op jit(solution)/shard_map/all_to_all | solution.py:210
  97.0 0.0 copy-start.1
  97.0 37.2 %all_to_all.21.got_ref = bf16[8,16,512]{2,1,0:T(8,128)(2,1)} all-to-all(bf16[8,16,512]{2,1,0:T(8,128)(2,1)} %bitcast.10), channel_id=1, replica_groups=mesh['y'=8,'core'=2,'x'=4,'zh'=2,'zl'=8] {'zl'}, dimensions={0} | all-to-all | bytes 262144 | tf_op jit(solution)/shard_map/all_to_all | solution.py:230
  134.1 0.0 all-gather.5.cloned.1.call-done
  134.1 0.0 copy-done.1
  134.1 4.2 %finish.1 = (bf16[112,512]{1,0:T(8,128)(2,1)}, bf16[112,512]{1,0:T(8,128)(2,1)}, bf16[16,512]{1,0:T(8,128)(2,1)}) custom-call(bf16[4,16,32,256]{3,2,1,0:T(8,128)(2,1)} %copy-done.1, bf16[16,4,32,512]{3,2,1,0:T(8,128)(2,1)} %bitcast.9, bf16[8,16,512]{2,1,0:T(8,128)(2,1)} %all_to_all.21.got_ref), custom_call_target="tpu_custom_call" | custom-call | tf_op jit(solution)/shard_map/finish/pallas_call | solution.py:231
Async XLA Ops:
  7.2 127.0 %all-gather.5.cloned.1.call-start = ((), (), s32[]{:S(2)}) async-start(), calls=%async_computation.4 | async-start | bytes 2228224 | tf_op jit(solution)/shard_map/all_gather | solution.py:179
  13.8 25.4 %copy-start = (bf16[16,1792]{1,0:T(8,128)(2,1)S(1)}, bf16[16,1792]{1,0:T(8,128)(2,1)}, u32[]{:S(2)}) copy-start(bf16[16,1792]{1,0:T(8,128)(2,1)} %cot_ref.1) | copy-start | bytes 172036
  56.6 21.0 %all-to-all-start.1 = ((bf16[16,32,256]{2,1,0:T(8,128)(2,1)}), bf16[16,32,256]{2,1,0:T(8,128)(2,1)S(1)}, u32[]{:S(2)}, u32[]{:S(2)}) async-start(bf16[16,32,256]{2,1,0:T(8,128)(2,1)} %get-tuple-element.16), calls=%async_computation.1 | async-start | bytes 524288 | tf_op jit(solution)/shard_map/all_to_all | solution.py:206
  78.8 18.2 %all-to-all-start.2 = ((bf16[4,16,32,256]{3,2,1,0:T(8,128)(2,1)}), bf16[4,16,32,256]{3,2,1,0:T(8,128)(2,1)S(1)}, u32[]{:S(2)}, u32[]{:S(2)}) async-start(bf16[4,16,32,256]{3,2,1,0:T(8,128)(2,1)} %broadcast_in_dim.2), calls=%async_computation.2 | async-start | bytes 2097152 | tf_op jit(solution)/shard_map/all_to_all | solution.py:210
  97.0 37.2 %copy-start.1 = (bf16[4,16,32,256]{3,2,1,0:T(8,128)(2,1)}, bf16[4,16,32,256]{3,2,1,0:T(8,128)(2,1)S(1)}, u32[]{:S(2)}) copy-start(bf16[4,16,32,256]{3,2,1,0:T(8,128)(2,1)S(1)} %all-to-all-done.2.dw_ref) | copy-start | bytes 3145732
Sparse Core Ops, SparseCore 0:
  13.9 55.1 all-gather.4

commit v3 on v1

v3 whole, which is shorter than its diff:
```python
import jax
import jax.numpy as jnp
from jax import lax
from jax.experimental import pallas as pl
from jax.experimental.pallas import tpu as pltpu
from jax.sharding import Mesh
from jax.sharding import PartitionSpec as P

GROUP = 128
CHUNK = 256
F32 = jnp.float32
BF16 = jnp.bfloat16


def dequant(q_ref, s_ref, j):
    rows = []
    for r in range(q_ref.shape[0] // GROUP):
        tiles = []
        for g in range(j * CHUNK // GROUP, (j + 1) * CHUNK // GROUP):
            tile = q_ref[r * GROUP : (r + 1) * GROUP, g * GROUP : (g + 1) * GROUP].astype(F32)
            tiles.append((tile * s_ref[r, g]).astype(BF16))
        rows.append(jnp.concatenate(tiles, axis=1))
    return jnp.concatenate(rows, axis=0)


def chunk_copies(q_refs, w_ref, sems):
    return [
        [
            pltpu.make_async_copy(
                q.at[:, pl.ds(j * CHUNK, CHUNK)], w_ref.at[t, :, pl.ds(j * CHUNK, CHUNK)], sems.at[t, j]
            )
            for t, q in enumerate(q_refs)
        ]
        for j in range(w_ref.shape[2] // CHUNK)
    ]


def forward_kernel(
    gs_ref, us_ref, act_ref, ast_ref, order_ref, gq_ref, uq_ref, pre_ref, nat_ref, w_ref, sems
):
    copies = chunk_copies((gq_ref, uq_ref), w_ref, sems)
    for pair in copies:
        for copy in pair:
            copy.start()
    tok, feat = act_ref.shape
    one_hot = (
        lax.broadcasted_iota(jnp.int32, (tok, tok), 0)
        == jnp.broadcast_to(order_ref[...], (tok, tok))
    ).astype(F32).astype(BF16)
    parts = []
    for g in range(feat // GROUP):
        scale = jnp.broadcast_to(ast_ref[g : g + 1, :], (tok, tok)).T
        part = act_ref[:, g * GROUP : (g + 1) * GROUP].astype(F32) * scale
        parts.append(part.astype(BF16))
    scaled = jnp.concatenate(parts, axis=1)
    natural = jnp.dot(one_hot, scaled, preferred_element_type=F32).astype(BF16)
    nat_ref[...] = natural
    for j, pair in enumerate(copies):
        for t, s_ref in enumerate((gs_ref, us_ref)):
            pair[t].wait()
            w = dequant(w_ref.at[t], s_ref, j)
            out = jnp.dot(natural, w, preferred_element_type=F32).astype(BF16)
            pre_ref[:, j, t] = out.reshape(pre_ref.shape[0], pre_ref.shape[3], CHUNK)


def reduce_kernel(got_ref, out_ref):
    for j in range(out_ref.shape[0]):
        for t in range(2):
            total = got_ref[0, j, t].astype(F32)
            for i in range(1, got_ref.shape[0]):
                total += got_ref[i, j, t].astype(F32)
            out_ref[j, t] = total.astype(BF16)


def activation_kernel(zh_ref, pre_ref, own_ref, other_ref, d_ref, dp_ref, dg_ref, du_ref):
    first = zh_ref[0] == 0
    for j in range(pre_ref.shape[1]):
        cols = slice(j * CHUNK, (j + 1) * CHUNK)
        own, other = own_ref[:, cols].astype(F32), other_ref[:, cols].astype(F32)
        cot = jnp.concatenate(
            [jnp.where(first, own, other), jnp.where(first, other, own)], axis=0
        )
        gate = pre_ref[0, j, 0].astype(F32) + pre_ref[1, j, 0].astype(F32)
        up = pre_ref[0, j, 1].astype(F32) + pre_ref[1, j, 1].astype(F32)
        s = jax.nn.sigmoid(gate)
        d_gate = (cot * up * s * (1.0 + gate * (1.0 - s))).astype(BF16)
        d_up = (cot * gate * s).astype(BF16)
        d_ref[j, 0] = d_gate
        d_ref[j, 1] = d_up
        dg_ref[:, cols] = d_gate.astype(F32)
        du_ref[:, cols] = d_up.astype(F32)
    parts, width = dp_ref.shape[0], dg_ref.shape[1]
    step = width // parts
    for k in range(parts):
        base = (k * step) // GROUP * GROUP
        span = min(2 * GROUP, width - base)
        shift = k * step - base
        for t, src in enumerate((dg_ref, du_ref)):
            window = src[:, base : base + span]
            if shift:
                window = pltpu.roll(window, span - shift, 1)
            dp_ref[k, :, t * GROUP : (t + 1) * GROUP] = window[:, :GROUP].astype(BF16)


def act_grad_kernel(gs_ref, us_ref, d_ref, gq_ref, uq_ref, out_ref, w_ref, sems):
    copies = chunk_copies((gq_ref, uq_ref), w_ref, sems)
    for pair in copies:
        for copy in pair:
            copy.start()
    total = None
    for j, pair in enumerate(copies):
        for t, s_ref in enumerate((gs_ref, us_ref)):
            pair[t].wait()
            w = dequant(w_ref.at[t], s_ref, j)
            rows = d_ref[:, j, t].reshape(out_ref.shape[0], CHUNK)
            part = lax.dot_general(rows, w, (((1,), (1,)), ((), ())), preferred_element_type=F32)
            total = part if total is None else total + part
    out_ref[...] = total.astype(BF16)


def finish_kernel(dw_ref, nat_ref, got_ref, gate_ref, up_ref, act_ref):
    total = None
    for k in range(dw_ref.shape[0]):
        rows = dw_ref[k].reshape(dw_ref.shape[1] * dw_ref.shape[2], dw_ref.shape[3])
        nat = nat_ref[:, k].reshape(rows.shape[0], nat_ref.shape[3])
        part = lax.dot_general(rows, nat, (((0,), (0,)), ((), ())), preferred_element_type=F32)
        total = part if total is None else total + part
    width = gate_ref.shape[0]
    gate_ref[...] = total[:width].astype(BF16)
    up_ref[...] = total[GROUP : GROUP + width].astype(BF16)
    act_ref[...] = sum(got_ref[i].astype(F32) for i in range(got_ref.shape[0])).astype(BF16)


def params(mib):
    return pltpu.CompilerParams(vmem_limit_bytes=mib * 1024 * 1024)


def on_device(
    act_values, activation_scale, token_order, gate_q, gate_scale, up_q, up_scale, cotangent
):
    n_x, n_zh = lax.axis_size("x"), lax.axis_size("zh")
    n_depth = lax.axis_size("y") * lax.axis_size("core")
    n_col = lax.axis_size("zl")
    tok, feat = act_values.shape
    hidden = gate_q.shape[1]
    n_chunks = hidden // CHUNK
    rows = tok // n_x
    slice_width = hidden // n_depth
    smem = pl.BlockSpec(memory_space=pltpu.SMEM)
    vmem = pl.BlockSpec(memory_space=pltpu.VMEM)
    hbm = pl.BlockSpec(memory_space=pltpu.HBM)
    weights_scratch = [
        pltpu.VMEM((2, feat, hidden), BF16),
        pltpu.SemaphoreType.DMA((2, n_chunks)),
    ]

    cot_other = lax.ppermute(cotangent, "zh", [(i, (i + 1) % n_zh) for i in range(n_zh)])
    zh = lax.axis_index("zh").astype(jnp.int32)[None]

    pre, natural = pl.pallas_call(
        forward_kernel,
        in_specs=[smem, smem, vmem, vmem, vmem, hbm, hbm],
        out_specs=[vmem, vmem],
        out_shape=[
            jax.ShapeDtypeStruct((n_x, n_chunks, 2, rows, CHUNK), BF16),
            jax.ShapeDtypeStruct((tok, feat), BF16),
        ],
        scratch_shapes=weights_scratch,
        compiler_params=params(60),
        name="forward",
    )(gate_scale, up_scale, act_values, activation_scale.T, token_order, gate_q, up_q)

    nat_all = lax.all_gather(natural, ("y", "core"), axis=0, tiled=False)
    nat_all = nat_all.reshape(n_depth, n_x, rows, feat)

    got = lax.all_to_all(pre, "x", 0, 0, tiled=True)
    part = pl.pallas_call(
        reduce_kernel,
        in_specs=[vmem],
        out_specs=vmem,
        out_shape=jax.ShapeDtypeStruct((n_chunks, 2, rows, CHUNK), BF16),
        compiler_params=params(16),
        name="reduce",
    )(got)
    both = lax.all_gather(part, "zh", axis=0, tiled=False)

    d, d_split = pl.pallas_call(
        activation_kernel,
        in_specs=[smem, vmem, vmem, vmem],
        out_specs=[vmem, vmem],
        out_shape=[
            jax.ShapeDtypeStruct((n_chunks, 2, rows, CHUNK), BF16),
            jax.ShapeDtypeStruct((n_depth, rows, 2 * GROUP), BF16),
        ],
        scratch_shapes=[pltpu.VMEM((rows, hidden), F32), pltpu.VMEM((rows, hidden), F32)],
        compiler_params=params(16),
        name="activation",
    )(zh, both, cotangent, cot_other)

    d_all = lax.all_gather(d, "x", axis=0, tiled=False)
    d_depth = lax.all_to_all(d_split, ("y", "core"), 0, 0, tiled=True)
    d_all, nat_all, d_depth = lax.optimization_barrier((d_all, nat_all, d_depth))

    act_part = pl.pallas_call(
        act_grad_kernel,
        in_specs=[smem, smem, vmem, hbm, hbm],
        out_specs=vmem,
        out_shape=jax.ShapeDtypeStruct((tok, feat), BF16),
        scratch_shapes=weights_scratch,
        compiler_params=params(60),
        name="act_grad",
    )(gate_scale, up_scale, d_all, gate_q, up_q)

    d_copies = jnp.broadcast_to(d_depth[None], (n_x,) + d_depth.shape)
    d_w = lax.all_to_all(d_copies, "x", 0, 0, tiled=True)
    act_part, d_w = lax.optimization_barrier((act_part, d_w))
    got_act = lax.all_to_all(act_part.reshape(n_col, tok // n_col, feat), "zl", 0, 0, tiled=True)
    gate_t, up_t, grad_act = pl.pallas_call(
        finish_kernel,
        in_specs=[vmem] * 3,
        out_specs=[vmem] * 3,
        out_shape=[
            jax.ShapeDtypeStruct((slice_width, feat), BF16),
            jax.ShapeDtypeStruct((slice_width, feat), BF16),
            jax.ShapeDtypeStruct((tok // n_col, feat), BF16),
        ],
        compiler_params=params(16),
        name="finish",
    )(d_w, nat_all, got_act)
    return grad_act, gate_t.T, up_t.T


def solution(mesh):
    sizes = mesh.shape
    n_zh, n_core = 2, 2
    fine = Mesh(
        mesh.devices.reshape(
            sizes["depth"] // n_core, n_core, sizes["row"] // n_zh, n_zh, sizes["col"]
        ),
        ("y", "core", "x", "zh", "zl"),
    )
    depth, row, col = ("y", "core"), ("x", "zh"), "zl"
    return jax.shard_map(
        on_device,
        mesh=fine,
        in_specs=(
            P(depth, row),
            P(depth, row),
            P(depth, None),
            P(row, col),
            P(row, col),
            P(row, col),
            P(row, col),
            P(depth + row, col),
        ),
        out_specs=(
            P(depth + (col,), row),
            P(row, (col,) + depth),
            P(row, (col,) + depth),
        ),
        check_vma=False,
    )
```

time: 145 us -> 138 us (0.952)
  the two profiles are of different devices: /device:TPU:11 before, /device:TPU:2 now
where the time goes in v3:
time: 138 us; the launch traced here: 137 us
  blocking collectives  64.1 us (46%)
  starting transfers between devices  36 us (26%)
  between operations  14.1 us (10%)
  Pallas kernels  13.5 us (10%)
  waiting for transfers between devices  8.18 us (6%)
    all_to_all x1, blocking collectives, on_device(): lax.all_to_all(act_part.reshape(n_col, tok // n_col, feat), 'zl', 0, 0, t...  31.8 us
    all_to_all x1, starting transfers between devices, on_device(): got = lax.all_to_all(pre, 'x', 0, 0, tiled=True)  16.7 us
    all_gather x1, blocking collectives, on_device(): both = lax.all_gather(part, 'zh', axis=0, tiled=False)  16.6 us
    all_gather x1, blocking collectives, on_device(): d_all = lax.all_gather(d, 'x', axis=0, tiled=False)  15.6 us
    ppermute x1, starting transfers between devices, on_device(): lax.ppermute(cotangent, 'zh', [(i, (i + 1) % n_zh) for i in range(n_zh)])  7.52 us
    all_to_all x1, starting transfers between devices, on_device(): d_depth = lax.all_to_all(d_split, ('y', 'core'), 0, 0, tiled=True)  7.27 us
    all_to_all x1, waiting for transfers between devices, on_device(): d_w = lax.all_to_all(d_copies, 'x', 0, 0, tiled=True)  6.96 us
    pallas_call x1, Pallas kernels, on_device(): pl.pallas_call(forward_kernel, in_specs=[smem, smem, vmem, vmem, vmem, hb...  6.08 us
  transfers between devices with their start and end apart: 5, of which 2 were waited for; matrix products, arithmetic and copies ran while one was open for 0% of the time, Pallas kernels for 4%

profile of v3, /device:TPU:2, one launch (start us, length us, event | category | flops | bytes accessed | tf_op | source)
XLA Modules:
  0.0 136.9 jit_solution(6426256014578581436)
XLA Ops:
  7.2 0.0 all-gather.5.cloned.1.call-start
  7.2 6.1 %forward.1 = (bf16[4,7,2,32,256]{4,3,2,1,0:T(8,128)(2,1)}, bf16[128,512]{1,0:T(8,128)(2,1)}) custom-call(f32[4,14]{1,0:T(4,128)} %gs_ref.3, f32[4,14]{1,0:T(4,128)} %us_ref.3, bf16[128,512]{1,0:T(8,128)(2,1)} %act_ref.1, f32[4,128]{1,0:T(4,128)} %bitcast.12, s32[1,128]{1,0:T(1,128)} %order_ref.1, bf16[512,1792]{1,0:T(8,128)(2,1)} %gq_ref.3, ...), custom_call_target="tpu_custom_call" | custom-call | tf_op jit(solution)/shard_map/forward/pallas_call | solution.py:160
  13.3 0.0 copy-start.1
  13.3 0.0 all-gather.5.cloned.1.call-update
  13.3 16.7 %all-to-all-start = ((bf16[4,7,2,32,256]{4,3,2,1,0:T(8,128)(2,1)}), bf16[4,7,2,32,256]{4,3,2,1,0:T(8,128)(2,1)S(1)}, u32[]{:S(2)}, u32[]{:S(2)}) async-start(bf16[4,7,2,32,256]{4,3,2,1,0:T(8,128)(2,1)} %get-tuple-element.15), calls=%async_computation | async-start | bytes 1835008 | tf_op jit(solution)/shard_map/all_to_all | solution.py:176
  30.0 0.0 copy-done.1
  30.0 7.5 %collective-permute-start = (bf16[16,1792]{1,0:T(8,128)(2,1)S(1)}, bf16[16,1792]{1,0:T(8,128)(2,1)S(1)}, u32[]{:S(2)}, u32[]{:S(2)}) collective-permute-start(bf16[16,1792]{1,0:T(8,128)(2,1)S(1)} %copy-done.1), channel_id=1, source_target_pairs={{0,8},{8,0},{1,9},{9,1},{2,10},{10,2},{3,11},{11,3},{4,12},{12,4},... | collective-permute-start | bytes 172040 | tf_op jit(solution)/shard_map/ppermute | solution.py:157
  37.5 1.2 all-to-all-done.got_ref
  38.7 0.1 reduce.1
  38.9 16.6 %all-gather = bf16[14,2,32,256]{3,2,1,0:T(8,128)(2,1)S(1)} all-gather(bf16[7,2,32,256]{3,2,1,0:T(8,128)(2,1)S(1)} %reduce.1), channel_id=2, replica_groups=mesh['y'=8,'core'=2,'x'=4,'zh'=2,'zl'=8] {'zh'}, dimensions={0}, use_global_device_ids=true | all-gather | bytes 688128 | tf_op jit(solution)/shard_map/all_gather | solution.py:185
  55.5 0.0 collective-permute-done.other_ref
  55.5 1.0 activation.1
  56.5 7.3 %all-to-all-start.1 = ((bf16[16,32,256]{2,1,0:T(8,128)(2,1)}), bf16[16,32,256]{2,1,0:T(8,128)(2,1)S(1)}, u32[]{:S(2)}, u32[]{:S(2)}) async-start(bf16[16,32,256]{2,1,0:T(8,128)(2,1)} %get-tuple-element.18), calls=%async_computation.1 | async-start | bytes 524288 | tf_op jit(solution)/shard_map/all_to_all | solution.py:201
  63.8 15.6 %all-gather.1 = bf16[28,2,32,256]{3,2,1,0:T(8,128)(2,1)} all-gather(bf16[7,2,32,256]{3,2,1,0:T(8,128)(2,1)S(1)} %get-tuple-element.16), channel_id=3, replica_groups=mesh['y'=8,'core'=2,'x'=4,'zh'=2,'zl'=8] {'x'}, dimensions={0}, use_global_device_ids=true | all-gather | bytes 1146880 | tf_op jit(solution)/shard_map/all_gather | solution.py:200
  79.4 0.0 all-to-all-done.1
  79.4 0.0 all-gather.5.cloned.1.call-done
  79.4 1.1 broadcast_in_dim.10
  80.5 4.5 %all-to-all-start.2 = ((bf16[4,16,32,256]{3,2,1,0:T(8,128)(2,1)}), bf16[4,16,32,256]{3,2,1,0:T(8,128)(2,1)S(1)}, u32[]{:S(2)}, u32[]{:S(2)}) async-start(bf16[4,16,32,256]{3,2,1,0:T(8,128)(2,1)} %broadcast_in_dim.10), calls=%async_computation.2 | async-start | bytes 2097152 | tf_op jit(solution)/shard_map/all_to_all | solution.py:215
  85.0 0.0 copy-start
  85.0 4.9 %act_grad.1 = bf16[128,512]{1,0:T(8,128)(2,1)} custom-call(f32[4,14]{1,0:T(4,128)} %gs_ref.3, f32[4,14]{1,0:T(4,128)} %us_ref.3, bf16[4,7,2,32,256]{4,3,2,1,0:T(8,128)(2,1)} %bitcast.10, bf16[512,1792]{1,0:T(8,128)(2,1)} %gq_ref.3, bf16[512,1792]{1,0:T(8,128)(2,1)} %uq_ref.3), custom_call_target="tpu_custom_call" | custom-call | tf_op jit(solution)/shard_map/act_grad/pallas_call | solution.py:204
  89.9 7.0 %all-to-all-done.2.dw_ref = bf16[4,16,32,256]{3,2,1,0:T(8,128)(2,1)S(1)} async-done(((bf16[4,16,32,256]{3,2,1,0:T(8,128)(2,1)}), bf16[4,16,32,256]{3,2,1,0:T(8,128)(2,1)S(1)}, u32[]{:S(2)}, u32[]{:S(2)}) %all-to-all-start.2) | async-done | bytes 1048608 | tf_op jit(solution)/shard_map/all_to_all | solution.py:215
  96.8 31.8 %all_to_all.20.got_ref = bf16[8,16,512]{2,1,0:T(8,128)(2,1)S(1)} all-to-all(bf16[8,16,512]{2,1,0:T(8,128)(2,1)} %bitcast.11), channel_id=1, replica_groups=mesh['y'=8,'core'=2,'x'=4,'zh'=2,'zl'=8] {'zl'}, dimensions={0} | all-to-all | bytes 262144 | tf_op jit(solution)/shard_map/all_to_all | solution.py:217
  128.6 0.0 copy-done
  128.7 1.4 %finish.1 = (bf16[112,512]{1,0:T(8,128)(2,1)}, bf16[112,512]{1,0:T(8,128)(2,1)}, bf16[16,512]{1,0:T(8,128)(2,1)}) custom-call(bf16[4,16,32,256]{3,2,1,0:T(8,128)(2,1)S(1)} %all-to-all-done.2.dw_ref, bf16[16,4,32,512]{3,2,1,0:T(8,128)(2,1)S(1)} %bitcast.8, bf16[8,16,512]{2,1,0:T(8,128)(2,1)S(1)} %all_to_all.20.got_ref), custom_call_target="tpu_custom_call" | custom-call | tf_op jit(solution)/shard_map/finish/pallas_call | solution.py:218
Async XLA Ops:
  7.2 72.2 %all-gather.5.cloned.1.call-start = ((), (), s32[]{:S(2)}) async-start(), calls=%async_computation.4 | async-start | bytes 2228224 | tf_op jit(solution)/shard_map/all_gather | solution.py:173
  13.3 16.7 %copy-start.1 = (bf16[16,1792]{1,0:T(8,128)(2,1)S(1)}, bf16[16,1792]{1,0:T(8,128)(2,1)}, u32[]{:S(2)}) copy-start(bf16[16,1792]{1,0:T(8,128)(2,1)} %own_ref.1) | copy-start | bytes 172036
  13.3 25.4 %all-to-all-start = ((bf16[4,7,2,32,256]{4,3,2,1,0:T(8,128)(2,1)}), bf16[4,7,2,32,256]{4,3,2,1,0:T(8,128)(2,1)S(1)}, u32[]{:S(2)}, u32[]{:S(2)}) async-start(bf16[4,7,2,32,256]{4,3,2,1,0:T(8,128)(2,1)} %get-tuple-element.15), calls=%async_computation | async-start | bytes 1835008 | tf_op jit(solution)/shard_map/all_to_all | solution.py:176
  30.0 25.5 %collective-permute-start = (bf16[16,1792]{1,0:T(8,128)(2,1)S(1)}, bf16[16,1792]{1,0:T(8,128)(2,1)S(1)}, u32[]{:S(2)}, u32[]{:S(2)}) collective-permute-start(bf16[16,1792]{1,0:T(8,128)(2,1)S(1)} %copy-done.1), channel_id=1, source_target_pairs={{0,8},{8,0},{1,9},{9,1},{2,10},{10,2},{3,11},{11,3},{4,12},{12,4},... | collective-permute-start | bytes 172040 | tf_op jit(solution)/shard_map/ppermute | solution.py:157
  56.5 22.9 %all-to-all-start.1 = ((bf16[16,32,256]{2,1,0:T(8,128)(2,1)}), bf16[16,32,256]{2,1,0:T(8,128)(2,1)S(1)}, u32[]{:S(2)}, u32[]{:S(2)}) async-start(bf16[16,32,256]{2,1,0:T(8,128)(2,1)} %get-tuple-element.18), calls=%async_computation.1 | async-start | bytes 524288 | tf_op jit(solution)/shard_map/all_to_all | solution.py:201
  80.5 16.4 %all-to-all-start.2 = ((bf16[4,16,32,256]{3,2,1,0:T(8,128)(2,1)}), bf16[4,16,32,256]{3,2,1,0:T(8,128)(2,1)S(1)}, u32[]{:S(2)}, u32[]{:S(2)}) async-start(bf16[4,16,32,256]{3,2,1,0:T(8,128)(2,1)} %broadcast_in_dim.10), calls=%async_computation.2 | async-start | bytes 2097152 | tf_op jit(solution)/shard_map/all_to_all | solution.py:215
  85.0 43.7 %copy-start = (bf16[2048,512]{1,0:T(8,128)(2,1)S(1)}, bf16[2048,512]{1,0:T(8,128)(2,1)}, u32[]{:S(2)}) copy-start(bf16[2048,512]{1,0:T(8,128)(2,1)} %all-gather.5.cloned.1.call-done) | copy-start | bytes 6291460
Sparse Core Ops, SparseCore 0:
  13.5 55.1 all-gather.4

commit v4 on v3

--- a/solution.py
+++ b/solution.py
@@ -8,6 +8,7 @@
 
 GROUP = 128
 CHUNK = 256
+AHEAD = 3
 F32 = jnp.float32
 BF16 = jnp.bfloat16
 
@@ -35,13 +36,40 @@
     ]
 
 
+def all_copies(pairs, sems):
+    copies = [pltpu.make_async_copy(src, dst, sems.at[i]) for i, (src, dst) in enumerate(pairs)]
+    start(copies)
+    return copies
+
+
+def start(copies):
+    for copy in copies:
+        copy.start()
+
+
+def wait(copies):
+    for copy in copies:
+        copy.wait()
+
+
 def forward_kernel(
-    gs_ref, us_ref, act_ref, ast_ref, order_ref, gq_ref, uq_ref, pre_ref, nat_ref, w_ref, sems
+    gs_hbm, us_hbm, act_hbm, ast_hbm, order_hbm, gq_ref, uq_ref, pre_ref, nat_ref,
+    gs_ref, us_ref, act_ref, ast_ref, order_ref, w_ref, sems, small_sems,
 ):
+    small = all_copies(
+        (
+            (act_hbm, act_ref),
+            (ast_hbm, ast_ref),
+            (order_hbm, order_ref),
+            (gs_hbm, gs_ref),
+            (us_hbm, us_ref),
+        ),
+        small_sems,
+    )
     copies = chunk_copies((gq_ref, uq_ref), w_ref, sems)
-    for pair in copies:
-        for copy in pair:
-            copy.start()
+    for pair in copies[:AHEAD]:
+        start(pair)
+    wait(small)
     tok, feat = act_ref.shape
     one_hot = (
         lax.broadcasted_iota(jnp.int32, (tok, tok), 0)
@@ -61,6 +89,8 @@
             w = dequant(w_ref.at[t], s_ref, j)
             out = jnp.dot(natural, w, preferred_element_type=F32).astype(BF16)
             pre_ref[:, j, t] = out.reshape(pre_ref.shape[0], pre_ref.shape[3], CHUNK)
+        if j + AHEAD < len(copies):
+            start(copies[j + AHEAD])
 
 
 def reduce_kernel(got_ref, out_ref):
@@ -102,13 +132,18 @@
             dp_ref[k, :, t * GROUP : (t + 1) * GROUP] = window[:, :GROUP].astype(BF16)
 
 
-def act_grad_kernel(gs_ref, us_ref, d_ref, gq_ref, uq_ref, out_ref, w_ref, sems):
+def act_grad_kernel(
+    gs_hbm, us_hbm, d_hbm, gq_ref, uq_ref, out_ref, gs_ref, us_ref, d_ref, w_ref, sems, small_sems
+):
+    small = all_copies(((gs_hbm, gs_ref), (us_hbm, us_ref)), small_sems)
     copies = chunk_copies((gq_ref, uq_ref), w_ref, sems)
-    for pair in copies:
-        for copy in pair:
-            copy.start()
+    for j, pair in enumerate(copies):
+        pair.append(pltpu.make_async_copy(d_hbm.at[:, j], d_ref.at[:, j], sems.at[2, j]))
+        start(pair)
+    wait(small)
     total = None
-    for j, pair in enumerate(copies):
+    for j, (*pair, d_copy) in enumerate(copies):
+        d_copy.wait()
         for t, s_ref in enumerate((gs_ref, us_ref)):
             pair[t].wait()
             w = dequant(w_ref.at[t], s_ref, j)
@@ -149,23 +184,29 @@
     smem = pl.BlockSpec(memory_space=pltpu.SMEM)
     vmem = pl.BlockSpec(memory_space=pltpu.VMEM)
     hbm = pl.BlockSpec(memory_space=pltpu.HBM)
-    weights_scratch = [
-        pltpu.VMEM((2, feat, hidden), BF16),
-        pltpu.SemaphoreType.DMA((2, n_chunks)),
-    ]
+    scale_scratch = [pltpu.SMEM(gate_scale.shape, F32), pltpu.SMEM(up_scale.shape, F32)]
+    weights_scratch = pltpu.VMEM((2, feat, hidden), BF16)
 
     cot_other = lax.ppermute(cotangent, "zh", [(i, (i + 1) % n_zh) for i in range(n_zh)])
     zh = lax.axis_index("zh").astype(jnp.int32)[None]
 
     pre, natural = pl.pallas_call(
         forward_kernel,
-        in_specs=[smem, smem, vmem, vmem, vmem, hbm, hbm],
+        in_specs=[hbm] * 7,
         out_specs=[vmem, vmem],
         out_shape=[
             jax.ShapeDtypeStruct((n_x, n_chunks, 2, rows, CHUNK), BF16),
             jax.ShapeDtypeStruct((tok, feat), BF16),
         ],
-        scratch_shapes=weights_scratch,
+        scratch_shapes=[
+            *scale_scratch,
+            pltpu.VMEM((tok, feat), BF16),
+            pltpu.VMEM((feat // GROUP, tok), F32),
+            pltpu.VMEM((1, tok), jnp.int32),
+            weights_scratch,
+            pltpu.SemaphoreType.DMA((2, n_chunks)),
+            pltpu.SemaphoreType.DMA((5,)),
+        ],
         compiler_params=params(60),
         name="forward",
     )(gate_scale, up_scale, act_values, activation_scale.T, token_order, gate_q, up_q)
@@ -203,10 +244,16 @@
 
     act_part = pl.pallas_call(
         act_grad_kernel,
-        in_specs=[smem, smem, vmem, hbm, hbm],
+        in_specs=[hbm] * 5,
         out_specs=vmem,
         out_shape=jax.ShapeDtypeStruct((tok, feat), BF16),
-        scratch_shapes=weights_scratch,
+        scratch_shapes=[
+            *scale_scratch,
+            pltpu.VMEM((n_x, n_chunks, 2, rows, CHUNK), BF16),
+            weights_scratch,
+            pltpu.SemaphoreType.DMA((3, n_chunks)),
+            pltpu.SemaphoreType.DMA((2,)),
+        ],
         compiler_params=params(60),
         name="act_grad",
     )(gate_scale, up_scale, d_all, gate_q, up_q)

time: 138 us -> 137 us (level)
  the two profiles are of different devices: /device:TPU:2 before, /device:TPU:8 now
where the time goes in v4:
time: 137 us
  blocking collectives  65 us (47%)
  starting transfers between devices  35.5 us (26%)
  between operations  14.1 us (10%)
  Pallas kernels  11.9 us (9%)
  waiting for transfers between devices  8.9 us (6%)
    all_to_all x1, blocking collectives, on_device(): lax.all_to_all(act_part.reshape(n_col, tok // n_col, feat), 'zl', 0, 0, t...  31.5 us
    ppermute x1, starting transfers between devices, on_device(): lax.ppermute(cotangent, 'zh', [(i, (i + 1) % n_zh) for i in range(n_zh)])  19.3 us
    all_gather x1, blocking collectives, on_device(): both = lax.all_gather(part, 'zh', axis=0, tiled=False)  18.6 us
    all_gather x1, blocking collectives, on_device(): d_all = lax.all_gather(d, 'x', axis=0, tiled=False)  14.8 us
    all_to_all x1, waiting for transfers between devices, on_device(): d_w = lax.all_to_all(d_copies, 'x', 0, 0, tiled=True)  8.87 us
    all_to_all x1, starting transfers between devices, on_device(): d_depth = lax.all_to_all(d_split, ('y', 'core'), 0, 0, tiled=True)  7.55 us
    pallas_call x1, Pallas kernels, on_device(): pl.pallas_call(forward_kernel, in_specs=[hbm] * 7, out_specs=[vmem, vmem]...  5.54 us
    all_to_all x1, starting transfers between devices, on_device(): got = lax.all_to_all(pre, 'x', 0, 0, tiled=True)  4.3 us
  transfers between devices with their start and end apart: 5, of which 1 were waited for; matrix products, arithmetic and copies ran while one was open for 0% of the time, Pallas kernels for 4%

profile of v4, /device:TPU:8, one launch (start us, length us, event | category | flops | bytes accessed | tf_op | source)
XLA Modules:
  0.0 136.5 jit_solution(16567854873094975296)
XLA Ops:
  7.2 0.0 all-gather.5.cloned.1.call-start
  7.2 5.5 %forward.1 = (bf16[4,7,2,32,256]{4,3,2,1,0:T(8,128)(2,1)}, bf16[128,512]{1,0:T(8,128)(2,1)}) custom-call(f32[4,14]{1,0:T(4,128)} %gs_hbm.3, f32[4,14]{1,0:T(4,128)} %us_hbm.3, bf16[128,512]{1,0:T(8,128)(2,1)} %act_hbm.1, f32[4,128]{1,0:T(4,128)} %bitcast.12, s32[1,128]{1,0:T(1,128)} %order_hbm.1, bf16[512,1792]{1,0:T(8,128)(2,1)} %gq_ref.3, ...), custom_call_target="tpu_custom_call" | custom-call | tf_op jit(solution)/shard_map/forward/pallas_call | solution.py:193
  12.8 0.0 copy-start.1
  12.8 0.0 all-gather.5.cloned.1.call-update
  12.8 4.3 %all-to-all-start = ((bf16[4,7,2,32,256]{4,3,2,1,0:T(8,128)(2,1)}), bf16[4,7,2,32,256]{4,3,2,1,0:T(8,128)(2,1)S(1)}, u32[]{:S(2)}, u32[]{:S(2)}) async-start(bf16[4,7,2,32,256]{4,3,2,1,0:T(8,128)(2,1)} %get-tuple-element.15), calls=%async_computation | async-start | bytes 1835008 | tf_op jit(solution)/shard_map/all_to_all | solution.py:217
  17.1 0.0 copy-done.1
  17.1 19.3 %collective-permute-start = (bf16[16,1792]{1,0:T(8,128)(2,1)S(1)}, bf16[16,1792]{1,0:T(8,128)(2,1)S(1)}, u32[]{:S(2)}, u32[]{:S(2)}) collective-permute-start(bf16[16,1792]{1,0:T(8,128)(2,1)S(1)} %copy-done.1), channel_id=1, source_target_pairs={{0,8},{8,0},{1,9},{9,1},{2,10},{10,2},{3,11},{11,3},{4,12},{12,4},... | collective-permute-start | bytes 172040 | tf_op jit(solution)/shard_map/ppermute | solution.py:190
  36.5 0.0 all-to-all-done.got_ref
  36.5 0.1 reduce.1
  36.6 18.6 %all-gather = bf16[14,2,32,256]{3,2,1,0:T(8,128)(2,1)S(1)} all-gather(bf16[7,2,32,256]{3,2,1,0:T(8,128)(2,1)S(1)} %reduce.1), channel_id=2, replica_groups=mesh['y'=8,'core'=2,'x'=4,'zh'=2,'zl'=8] {'zh'}, dimensions={0}, use_global_device_ids=true | all-gather | bytes 688128 | tf_op jit(solution)/shard_map/all_gather | solution.py:226
  55.2 0.0 collective-permute-done.other_ref
  55.2 1.0 activation.1
  56.2 7.6 %all-to-all-start.1 = ((bf16[16,32,256]{2,1,0:T(8,128)(2,1)}), bf16[16,32,256]{2,1,0:T(8,128)(2,1)S(1)}, u32[]{:S(2)}, u32[]{:S(2)}) async-start(bf16[16,32,256]{2,1,0:T(8,128)(2,1)} %get-tuple-element.18), calls=%async_computation.1 | async-start | bytes 524288 | tf_op jit(solution)/shard_map/all_to_all | solution.py:242
  63.8 14.8 %all-gather.1 = bf16[28,2,32,256]{3,2,1,0:T(8,128)(2,1)} all-gather(bf16[7,2,32,256]{3,2,1,0:T(8,128)(2,1)S(1)} %get-tuple-element.16), channel_id=3, replica_groups=mesh['y'=8,'core'=2,'x'=4,'zh'=2,'zl'=8] {'x'}, dimensions={0}, use_global_device_ids=true | all-gather | bytes 1146880 | tf_op jit(solution)/shard_map/all_gather | solution.py:241
  78.6 0.0 all-to-all-done.1
  78.6 0.0 all-gather.5.cloned.1.call-done
  78.6 1.1 broadcast_in_dim.10
  79.7 4.3 %all-to-all-start.2 = ((bf16[4,16,32,256]{3,2,1,0:T(8,128)(2,1)}), bf16[4,16,32,256]{3,2,1,0:T(8,128)(2,1)S(1)}, u32[]{:S(2)}, u32[]{:S(2)}) async-start(bf16[4,16,32,256]{3,2,1,0:T(8,128)(2,1)} %broadcast_in_dim.10), calls=%async_computation.2 | async-start | bytes 2097152 | tf_op jit(solution)/shard_map/all_to_all | solution.py:262
  84.0 0.0 copy-start
  84.0 3.9 %act_grad.1 = bf16[128,512]{1,0:T(8,128)(2,1)} custom-call(f32[4,14]{1,0:T(4,128)} %gs_hbm.3, f32[4,14]{1,0:T(4,128)} %us_hbm.3, bf16[4,7,2,32,256]{4,3,2,1,0:T(8,128)(2,1)} %bitcast.10, bf16[512,1792]{1,0:T(8,128)(2,1)} %gq_ref.3, bf16[512,1792]{1,0:T(8,128)(2,1)} %uq_ref.3), custom_call_target="tpu_custom_call" | custom-call | tf_op jit(solution)/shard_map/act_grad/pallas_call | solution.py:245
  87.9 8.9 %all-to-all-done.2.dw_ref = bf16[4,16,32,256]{3,2,1,0:T(8,128)(2,1)S(1)} async-done(((bf16[4,16,32,256]{3,2,1,0:T(8,128)(2,1)}), bf16[4,16,32,256]{3,2,1,0:T(8,128)(2,1)S(1)}, u32[]{:S(2)}, u32[]{:S(2)}) %all-to-all-start.2) | async-done | bytes 1048608 | tf_op jit(solution)/shard_map/all_to_all | solution.py:262
  96.8 31.5 %all_to_all.20.got_ref = bf16[8,16,512]{2,1,0:T(8,128)(2,1)S(1)} all-to-all(bf16[8,16,512]{2,1,0:T(8,128)(2,1)} %bitcast.11), channel_id=1, replica_groups=mesh['y'=8,'core'=2,'x'=4,'zh'=2,'zl'=8] {'zl'}, dimensions={0} | all-to-all | bytes 262144 | tf_op jit(solution)/shard_map/all_to_all | solution.py:264
  128.3 0.0 copy-done
  128.3 1.4 %finish.1 = (bf16[112,512]{1,0:T(8,128)(2,1)}, bf16[112,512]{1,0:T(8,128)(2,1)}, bf16[16,512]{1,0:T(8,128)(2,1)}) custom-call(bf16[4,16,32,256]{3,2,1,0:T(8,128)(2,1)S(1)} %all-to-all-done.2.dw_ref, bf16[16,4,32,512]{3,2,1,0:T(8,128)(2,1)S(1)} %bitcast.8, bf16[8,16,512]{2,1,0:T(8,128)(2,1)S(1)} %all_to_all.20.got_ref), custom_call_target="tpu_custom_call" | custom-call | tf_op jit(solution)/shard_map/finish/pallas_call | solution.py:265
Async XLA Ops:
  7.2 71.4 %all-gather.5.cloned.1.call-start = ((), (), s32[]{:S(2)}) async-start(), calls=%async_computation.4 | async-start | bytes 2228224 | tf_op jit(solution)/shard_map/all_gather | solution.py:214
  12.8 4.3 %copy-start.1 = (bf16[16,1792]{1,0:T(8,128)(2,1)S(1)}, bf16[16,1792]{1,0:T(8,128)(2,1)}, u32[]{:S(2)}) copy-start(bf16[16,1792]{1,0:T(8,128)(2,1)} %own_ref.1) | copy-start | bytes 172036
  12.8 23.7 %all-to-all-start = ((bf16[4,7,2,32,256]{4,3,2,1,0:T(8,128)(2,1)}), bf16[4,7,2,32,256]{4,3,2,1,0:T(8,128)(2,1)S(1)}, u32[]{:S(2)}, u32[]{:S(2)}) async-start(bf16[4,7,2,32,256]{4,3,2,1,0:T(8,128)(2,1)} %get-tuple-element.15), calls=%async_computation | async-start | bytes 1835008 | tf_op jit(solution)/shard_map/all_to_all | solution.py:217
  17.1 38.1 %collective-permute-start = (bf16[16,1792]{1,0:T(8,128)(2,1)S(1)}, bf16[16,1792]{1,0:T(8,128)(2,1)S(1)}, u32[]{:S(2)}, u32[]{:S(2)}) collective-permute-start(bf16[16,1792]{1,0:T(8,128)(2,1)S(1)} %copy-done.1), channel_id=1, source_target_pairs={{0,8},{8,0},{1,9},{9,1},{2,10},{10,2},{3,11},{11,3},{4,12},{12,4},... | collective-permute-start | bytes 172040 | tf_op jit(solution)/shard_map/ppermute | solution.py:190
  56.2 22.4 %all-to-all-start.1 = ((bf16[16,32,256]{2,1,0:T(8,128)(2,1)}), bf16[16,32,256]{2,1,0:T(8,128)(2,1)S(1)}, u32[]{:S(2)}, u32[]{:S(2)}) async-start(bf16[16,32,256]{2,1,0:T(8,128)(2,1)} %get-tuple-element.18), calls=%async_computation.1 | async-start | bytes 524288 | tf_op jit(solution)/shard_map/all_to_all | solution.py:242
  79.7 17.1 %all-to-all-start.2 = ((bf16[4,16,32,256]{3,2,1,0:T(8,128)(2,1)}), bf16[4,16,32,256]{3,2,1,0:T(8,128)(2,1)S(1)}, u32[]{:S(2)}, u32[]{:S(2)}) async-start(bf16[4,16,32,256]{3,2,1,0:T(8,128)(2,1)} %broadcast_in_dim.10), calls=%async_computation.2 | async-start | bytes 2097152 | tf_op jit(solution)/shard_map/all_to_all | solution.py:262
  84.0 44.3 %copy-start = (bf16[2048,512]{1,0:T(8,128)(2,1)S(1)}, bf16[2048,512]{1,0:T(8,128)(2,1)}, u32[]{:S(2)}) copy-start(bf16[2048,512]{1,0:T(8,128)(2,1)} %all-gather.5.cloned.1.call-done) | copy-start | bytes 6291460
Sparse Core Ops, SparseCore 0:
  12.9 55.3 all-gather.4

commit v5 on v4

--- a/solution.py
+++ b/solution.py
@@ -241,6 +241,7 @@
     d_all = lax.all_gather(d, "x", axis=0, tiled=False)
     d_depth = lax.all_to_all(d_split, ("y", "core"), 0, 0, tiled=True)
     d_all, nat_all, d_depth = lax.optimization_barrier((d_all, nat_all, d_depth))
+    d_w = lax.all_gather(d_depth, "x", axis=0, tiled=False)
 
     act_part = pl.pallas_call(
         act_grad_kernel,
@@ -258,9 +259,6 @@
         name="act_grad",
     )(gate_scale, up_scale, d_all, gate_q, up_q)
 
-    d_copies = jnp.broadcast_to(d_depth[None], (n_x,) + d_depth.shape)
-    d_w = lax.all_to_all(d_copies, "x", 0, 0, tiled=True)
-    act_part, d_w = lax.optimization_barrier((act_part, d_w))
     got_act = lax.all_to_all(act_part.reshape(n_col, tok // n_col, feat), "zl", 0, 0, tiled=True)
     gate_t, up_t, grad_act = pl.pallas_call(
         finish_kernel,

time: 137 us -> 137 us (level)
  the two profiles are of different devices: /device:TPU:8 before, /device:TPU:2 now
where the time goes in v5:
time: 137 us; the launch traced here: 136 us
  blocking collectives  63.6 us (46%)
  starting transfers between devices  31.5 us (23%)
  between operations  14.1 us (10%)
  waiting for transfers between devices  12.9 us (9%)
  Pallas kernels  11.9 us (9%)
  local copies, waits for them, and re-layouts  1.91 us (1%)
    all_to_all x1, blocking collectives, on_device(): lax.all_to_all(act_part.reshape(n_col, tok // n_col, feat), 'zl', 0, 0, t...  31.4 us
    all_to_all x1, starting transfers between devices, on_device(): got = lax.all_to_all(pre, 'x', 0, 0, tiled=True)  16.7 us
    all_gather x1, blocking collectives, on_device(): both = lax.all_gather(part, 'zh', axis=0, tiled=False)  16.7 us
    all_gather x1, blocking collectives, on_device(): d_all = lax.all_gather(d, 'x', axis=0, tiled=False)  15.6 us
    all_gather x1, waiting for transfers between devices, on_device(): d_w = lax.all_gather(d_depth, 'x', axis=0, tiled=False)  11.6 us
    ppermute x1, starting transfers between devices, on_device(): lax.ppermute(cotangent, 'zh', [(i, (i + 1) % n_zh) for i in range(n_zh)])  7.52 us
    all_to_all x1, starting transfers between devices, on_device(): d_depth = lax.all_to_all(d_split, ('y', 'core'), 0, 0, tiled=True)  7.25 us
    pallas_call x1, Pallas kernels, on_device(): pl.pallas_call(forward_kernel, in_specs=[hbm] * 7, out_specs=[vmem, vmem]...  5.52 us
  transfers between devices with their start and end apart: 5, of which 2 were waited for; matrix products, arithmetic and copies ran while one was open for 0% of the time, Pallas kernels for 4%

profile of v5, /device:TPU:2, one launch (start us, length us, event | category | flops | bytes accessed | tf_op | source)
XLA Modules:
  0.0 136.0 jit_solution(5958878838365010878)
XLA Ops:
  7.2 0.0 all-gather.7.cloned.1.call-start
  7.2 5.5 %forward.1 = (bf16[4,7,2,32,256]{4,3,2,1,0:T(8,128)(2,1)}, bf16[128,512]{1,0:T(8,128)(2,1)}) custom-call(f32[4,14]{1,0:T(4,128)} %gs_hbm.3, f32[4,14]{1,0:T(4,128)} %us_hbm.3, bf16[128,512]{1,0:T(8,128)(2,1)} %act_hbm.1, f32[4,128]{1,0:T(4,128)} %bitcast.14, s32[1,128]{1,0:T(1,128)} %order_hbm.1, bf16[512,1792]{1,0:T(8,128)(2,1)} %gq_ref.3, ...), custom_call_target="tpu_custom_call" | custom-call | tf_op jit(solution)/shard_map/forward/pallas_call | solution.py:193
  12.7 0.0 copy-start.2
  12.7 0.0 all-gather.7.cloned.1.call-update
  12.8 16.7 %all-to-all-start = ((bf16[4,7,2,32,256]{4,3,2,1,0:T(8,128)(2,1)}), bf16[4,7,2,32,256]{4,3,2,1,0:T(8,128)(2,1)S(1)}, u32[]{:S(2)}, u32[]{:S(2)}) async-start(bf16[4,7,2,32,256]{4,3,2,1,0:T(8,128)(2,1)} %get-tuple-element.13), calls=%async_computation | async-start | bytes 1835008 | tf_op jit(solution)/shard_map/all_to_all | solution.py:217
  29.4 0.0 copy-done.2
  29.4 7.5 %collective-permute-start = (bf16[16,1792]{1,0:T(8,128)(2,1)S(1)}, bf16[16,1792]{1,0:T(8,128)(2,1)S(1)}, u32[]{:S(2)}, u32[]{:S(2)}) collective-permute-start(bf16[16,1792]{1,0:T(8,128)(2,1)S(1)} %copy-done.2), channel_id=1, source_target_pairs={{0,8},{8,0},{1,9},{9,1},{2,10},{10,2},{3,11},{11,3},{4,12},{12,4},... | collective-permute-start | bytes 172040 | tf_op jit(solution)/shard_map/ppermute | solution.py:190
  37.0 1.2 all-to-all-done.got_ref
  38.2 0.1 reduce.1
  38.3 16.7 %all-gather = bf16[14,2,32,256]{3,2,1,0:T(8,128)(2,1)S(1)} all-gather(bf16[7,2,32,256]{3,2,1,0:T(8,128)(2,1)S(1)} %reduce.1), channel_id=2, replica_groups=mesh['y'=8,'core'=2,'x'=4,'zh'=2,'zl'=8] {'zh'}, dimensions={0}, use_global_device_ids=true | all-gather | bytes 688128 | tf_op jit(solution)/shard_map/all_gather | solution.py:226
  55.0 0.0 collective-permute-done.other_ref
  55.0 1.0 activation.1
  55.9 7.3 %all-to-all-start.1 = ((bf16[16,32,256]{2,1,0:T(8,128)(2,1)}), bf16[16,32,256]{2,1,0:T(8,128)(2,1)S(1)}, u32[]{:S(2)}, u32[]{:S(2)}) async-start(bf16[16,32,256]{2,1,0:T(8,128)(2,1)} %get-tuple-element.16), calls=%async_computation.1 | async-start | bytes 524288 | tf_op jit(solution)/shard_map/all_to_all | solution.py:242
  63.2 0.0 all-gather.9.cloned.1.call-start
  63.2 15.6 %all-gather.1 = bf16[28,2,32,256]{3,2,1,0:T(8,128)(2,1)} all-gather(bf16[7,2,32,256]{3,2,1,0:T(8,128)(2,1)S(1)} %get-tuple-element.14), channel_id=3, replica_groups=mesh['y'=8,'core'=2,'x'=4,'zh'=2,'zl'=8] {'x'}, dimensions={0}, use_global_device_ids=true | all-gather | bytes 1146880 | tf_op jit(solution)/shard_map/all_gather | solution.py:241
  78.8 0.0 all-to-all-done.1
  78.9 0.0 copy-start.3
  78.9 0.0 all-gather.7.cloned.1.call-done
  78.9 0.7 copy-done.3
  79.6 0.0 all-gather.9.cloned.1.call-update
  79.6 0.0 copy-start
  79.6 3.9 %act_grad.1 = bf16[128,512]{1,0:T(8,128)(2,1)} custom-call(f32[4,14]{1,0:T(4,128)} %gs_hbm.3, f32[4,14]{1,0:T(4,128)} %us_hbm.3, bf16[4,7,2,32,256]{4,3,2,1,0:T(8,128)(2,1)} %bitcast.12, bf16[512,1792]{1,0:T(8,128)(2,1)} %gq_ref.3, bf16[512,1792]{1,0:T(8,128)(2,1)} %uq_ref.3), custom_call_target="tpu_custom_call" | custom-call | tf_op jit(solution)/shard_map/act_grad/pallas_call | solution.py:246
  83.5 31.4 %all_to_all.15.got_ref = bf16[8,16,512]{2,1,0:T(8,128)(2,1)S(1)} all-to-all(bf16[8,16,512]{2,1,0:T(8,128)(2,1)} %bitcast.13), channel_id=1, replica_groups=mesh['y'=8,'core'=2,'x'=4,'zh'=2,'zl'=8] {'zl'}, dimensions={0} | all-to-all | bytes 262144 | tf_op jit(solution)/shard_map/all_to_all | solution.py:262
  114.9 11.6 %all-gather.9.cloned.1.call-done = bf16[64,32,256]{2,1,0:T(8,128)(2,1)} async-done(((bf16[16,32,256]{2,1,0:T(8,128)(2,1)}), bf16[64,32,256]{2,1,0:T(8,128)(2,1)}) %all-gather.9.cloned.1.call-update) | async-done | bytes 1048592 | tf_op jit(solution)/shard_map/all_gather | solution.py:244
  126.5 0.0 copy-done
  126.5 0.0 copy-start.1
  126.5 1.2 copy-done.1
  127.7 1.4 %finish.1 = (bf16[112,512]{1,0:T(8,128)(2,1)}, bf16[112,512]{1,0:T(8,128)(2,1)}, bf16[16,512]{1,0:T(8,128)(2,1)}) custom-call(bf16[4,16,32,256]{3,2,1,0:T(8,128)(2,1)S(1)} %bitcast.11, bf16[16,4,32,512]{3,2,1,0:T(8,128)(2,1)S(1)} %bitcast.9, bf16[8,16,512]{2,1,0:T(8,128)(2,1)S(1)} %all_to_all.15.got_ref), custom_call_target="tpu_custom_call" | custom-call | tf_op jit(solution)/shard_map/finish/pallas_call | solution.py:263
Async XLA Ops:
  7.2 71.7 %all-gather.7.cloned.1.call-start = ((), (), s32[]{:S(2)}) async-start(), calls=%async_computation.3 | async-start | bytes 2228224 | tf_op jit(solution)/shard_map/all_gather | solution.py:214
  12.7 16.7 %copy-start.2 = (bf16[16,1792]{1,0:T(8,128)(2,1)S(1)}, bf16[16,1792]{1,0:T(8,128)(2,1)}, u32[]{:S(2)}) copy-start(bf16[16,1792]{1,0:T(8,128)(2,1)} %own_ref.1) | copy-start | bytes 172036
  12.8 25.4 %all-to-all-start = ((bf16[4,7,2,32,256]{4,3,2,1,0:T(8,128)(2,1)}), bf16[4,7,2,32,256]{4,3,2,1,0:T(8,128)(2,1)S(1)}, u32[]{:S(2)}, u32[]{:S(2)}) async-start(bf16[4,7,2,32,256]{4,3,2,1,0:T(8,128)(2,1)} %get-tuple-element.13), calls=%async_computation | async-start | bytes 1835008 | tf_op jit(solution)/shard_map/all_to_all | solution.py:217
  29.4 25.5 %collective-permute-start = (bf16[16,1792]{1,0:T(8,128)(2,1)S(1)}, bf16[16,1792]{1,0:T(8,128)(2,1)S(1)}, u32[]{:S(2)}, u32[]{:S(2)}) collective-permute-start(bf16[16,1792]{1,0:T(8,128)(2,1)S(1)} %copy-done.2), channel_id=1, source_target_pairs={{0,8},{8,0},{1,9},{9,1},{2,10},{10,2},{3,11},{11,3},{4,12},{12,4},... | collective-permute-start | bytes 172040 | tf_op jit(solution)/shard_map/ppermute | solution.py:190
  55.9 22.9 %all-to-all-start.1 = ((bf16[16,32,256]{2,1,0:T(8,128)(2,1)}), bf16[16,32,256]{2,1,0:T(8,128)(2,1)S(1)}, u32[]{:S(2)}, u32[]{:S(2)}) async-start(bf16[16,32,256]{2,1,0:T(8,128)(2,1)} %get-tuple-element.16), calls=%async_computation.1 | async-start | bytes 524288 | tf_op jit(solution)/shard_map/all_to_all | solution.py:242
  63.2 63.3 %all-gather.9.cloned.1.call-start = ((), (), s32[]{:S(2)}) async-start(), calls=%async_computation.4 | async-start | bytes 1310720 | tf_op jit(solution)/shard_map/all_gather | solution.py:244
  78.9 0.7 copy-start.3
  79.6 46.9 %copy-start = (bf16[2048,512]{1,0:T(8,128)(2,1)S(1)}, bf16[2048,512]{1,0:T(8,128)(2,1)}, u32[]{:S(2)}) copy-start(bf16[2048,512]{1,0:T(8,128)(2,1)} %all-gather.7.cloned.1.call-done) | copy-start | bytes 6291460
  126.5 1.2 copy-start.1
Sparse Core Ops, SparseCore 0:
  12.9 55.1 all-gather.6
  79.7 46.7 all-gather.8

commit v6 on v4

--- a/solution.py
+++ b/solution.py
@@ -240,7 +240,7 @@
 
     d_all = lax.all_gather(d, "x", axis=0, tiled=False)
     d_depth = lax.all_to_all(d_split, ("y", "core"), 0, 0, tiled=True)
-    d_all, nat_all, d_depth = lax.optimization_barrier((d_all, nat_all, d_depth))
+    d_all, nat_all = lax.optimization_barrier((d_all, nat_all))
 
     act_part = pl.pallas_call(
         act_grad_kernel,
@@ -260,7 +260,6 @@
 
     d_copies = jnp.broadcast_to(d_depth[None], (n_x,) + d_depth.shape)
     d_w = lax.all_to_all(d_copies, "x", 0, 0, tiled=True)
-    act_part, d_w = lax.optimization_barrier((act_part, d_w))
     got_act = lax.all_to_all(act_part.reshape(n_col, tok // n_col, feat), "zl", 0, 0, tiled=True)
     gate_t, up_t, grad_act = pl.pallas_call(
         finish_kernel,

time: 137 us -> 148 us (1.080)
  the two profiles are of different devices: /device:TPU:8 before, /device:TPU:64 now
where the time goes in v6:
time: 148 us; the launch traced here: 147 us
  blocking collectives  94.7 us (64%)
  starting transfers between devices  26.3 us (18%)
  between operations  14.1 us (10%)
  Pallas kernels  11.2 us (8%)
    all_gather x1, blocking collectives, on_device(): both = lax.all_gather(part, 'zh', axis=0, tiled=False)  31.8 us
    all_gather x1, blocking collectives, on_device(): d_all = lax.all_gather(d, 'x', axis=0, tiled=False)  26.6 us
    ppermute x1, starting transfers between devices, on_device(): lax.ppermute(cotangent, 'zh', [(i, (i + 1) % n_zh) for i in range(n_zh)])  18.4 us
    all_to_all x1, blocking collectives, on_device(): d_depth = lax.all_to_all(d_split, ('y', 'core'), 0, 0, tiled=True)  18.2 us
    all_to_all x1, blocking collectives, on_device(): lax.all_to_all(act_part.reshape(n_col, tok // n_col, feat), 'zl', 0, 0, t...  18.1 us
    pallas_call x1, Pallas kernels, on_device(): pl.pallas_call(forward_kernel, in_specs=[hbm] * 7, out_specs=[vmem, vmem]...  5.53 us
    all_to_all x1, starting transfers between devices, on_device(): got = lax.all_to_all(pre, 'x', 0, 0, tiled=True)  4.31 us
    pallas_call x1, Pallas kernels, on_device(): pl.pallas_call(act_grad_kernel, in_specs=[hbm] * 5, out_specs=vmem, out_s...  3.88 us
  transfers between devices with their start and end apart: 4, of which 0 were waited for; matrix products, arithmetic and copies ran while one was open for 1% of the time, Pallas kernels for 3%

profile of v6, /device:TPU:64, one launch (start us, length us, event | category | flops | bytes accessed | tf_op | source)
XLA Modules:
  0.0 147.5 jit_solution(5390702095072762373)
XLA Ops:
  7.2 0.0 all-gather.5.cloned.1.call-start
  7.2 5.5 %forward.1 = (bf16[4,7,2,32,256]{4,3,2,1,0:T(8,128)(2,1)}, bf16[128,512]{1,0:T(8,128)(2,1)}) custom-call(f32[4,14]{1,0:T(4,128)} %gs_hbm.3, f32[4,14]{1,0:T(4,128)} %us_hbm.3, bf16[128,512]{1,0:T(8,128)(2,1)} %act_hbm.1, f32[4,128]{1,0:T(4,128)} %bitcast.12, s32[1,128]{1,0:T(1,128)} %order_hbm.1, bf16[512,1792]{1,0:T(8,128)(2,1)} %gq_ref.3, ...), custom_call_target="tpu_custom_call" | custom-call | tf_op jit(solution)/shard_map/forward/pallas_call | solution.py:193
  12.7 0.0 copy-start.1
  12.8 0.0 all-gather.5.cloned.1.call-update
  12.8 4.3 %all-to-all-start = ((bf16[4,7,2,32,256]{4,3,2,1,0:T(8,128)(2,1)}), bf16[4,7,2,32,256]{4,3,2,1,0:T(8,128)(2,1)S(1)}, u32[]{:S(2)}, u32[]{:S(2)}) async-start(bf16[4,7,2,32,256]{4,3,2,1,0:T(8,128)(2,1)} %get-tuple-element.12), calls=%async_computation | async-start | bytes 1835008 | tf_op jit(solution)/shard_map/all_to_all | solution.py:217
  17.1 0.0 copy-done.1
  17.1 18.4 %collective-permute-start = (bf16[16,1792]{1,0:T(8,128)(2,1)S(1)}, bf16[16,1792]{1,0:T(8,128)(2,1)S(1)}, u32[]{:S(2)}, u32[]{:S(2)}) collective-permute-start(bf16[16,1792]{1,0:T(8,128)(2,1)S(1)} %copy-done.1), channel_id=1, source_target_pairs={{0,8},{8,0},{1,9},{9,1},{2,10},{10,2},{3,11},{11,3},{4,12},{12,4},... | collective-permute-start | bytes 172040 | tf_op jit(solution)/shard_map/ppermute | solution.py:190
  35.6 0.0 all-to-all-done.got_ref
  35.6 0.1 reduce.1
  35.7 31.8 %all-gather = bf16[14,2,32,256]{3,2,1,0:T(8,128)(2,1)S(1)} all-gather(bf16[7,2,32,256]{3,2,1,0:T(8,128)(2,1)S(1)} %reduce.1), channel_id=2, replica_groups=mesh['y'=8,'core'=2,'x'=4,'zh'=2,'zl'=8] {'zh'}, dimensions={0}, use_global_device_ids=true | all-gather | bytes 688128 | tf_op jit(solution)/shard_map/all_gather | solution.py:226
  67.5 0.0 collective-permute-done.other_ref
  67.5 0.3 activation.1
  67.8 18.2 %all_to_all.20 = bf16[16,32,256]{2,1,0:T(8,128)(2,1)S(1)} all-to-all(bf16[16,32,256]{2,1,0:T(8,128)(2,1)S(1)} %get-tuple-element.13), channel_id=1, replica_groups=mesh['y'=8,'core'=2,'x'=4,'zh'=2,'zl'=8] {'y','core'}, dimensions={0} | all-to-all | bytes 524288 | tf_op jit(solution)/shard_map/all_to_all | solution.py:242
  86.0 1.1 broadcast_in_dim.10
  87.1 3.5 %all-to-all-start.2 = ((bf16[4,16,32,256]{3,2,1,0:T(8,128)(2,1)}), bf16[4,16,32,256]{3,2,1,0:T(8,128)(2,1)S(1)}, u32[]{:S(2)}, u32[]{:S(2)}) async-start(bf16[4,16,32,256]{3,2,1,0:T(8,128)(2,1)} %broadcast_in_dim.10), calls=%async_computation.2 | async-start | bytes 2097152 | tf_op jit(solution)/shard_map/all_to_all | solution.py:262
  90.6 26.6 %all-gather.1 = bf16[28,2,32,256]{3,2,1,0:T(8,128)(2,1)} all-gather(bf16[7,2,32,256]{3,2,1,0:T(8,128)(2,1)S(1)} %get-tuple-element.14), channel_id=3, replica_groups=mesh['y'=8,'core'=2,'x'=4,'zh'=2,'zl'=8] {'x'}, dimensions={0}, use_global_device_ids=true | all-gather | bytes 1146880 | tf_op jit(solution)/shard_map/all_gather | solution.py:241
  117.2 0.0 all-gather.5.cloned.1.call-done
  117.2 0.0 copy-start
  117.2 3.9 %act_grad.1 = bf16[128,512]{1,0:T(8,128)(2,1)} custom-call(f32[4,14]{1,0:T(4,128)} %gs_hbm.3, f32[4,14]{1,0:T(4,128)} %us_hbm.3, bf16[4,7,2,32,256]{4,3,2,1,0:T(8,128)(2,1)} %bitcast.10, bf16[512,1792]{1,0:T(8,128)(2,1)} %gq_ref.3, bf16[512,1792]{1,0:T(8,128)(2,1)} %uq_ref.3), custom_call_target="tpu_custom_call" | custom-call | tf_op jit(solution)/shard_map/act_grad/pallas_call | solution.py:245
  121.1 0.0 all-to-all-done.2.dw_ref
  121.1 18.1 %all_to_all.21.got_ref = bf16[8,16,512]{2,1,0:T(8,128)(2,1)S(1)} all-to-all(bf16[8,16,512]{2,1,0:T(8,128)(2,1)} %bitcast.11), channel_id=1, replica_groups=mesh['y'=8,'core'=2,'x'=4,'zh'=2,'zl'=8] {'zl'}, dimensions={0} | all-to-all | bytes 262144 | tf_op jit(solution)/shard_map/all_to_all | solution.py:263
  139.2 0.0 copy-done
  139.2 1.4 finish.1
Async XLA Ops:
  7.2 110.0 %all-gather.5.cloned.1.call-start = ((), (), s32[]{:S(2)}) async-start(), calls=%async_computation.4 | async-start | bytes 2228224 | tf_op jit(solution)/shard_map/all_gather | solution.py:214
  12.7 4.3 %copy-start.1 = (bf16[16,1792]{1,0:T(8,128)(2,1)S(1)}, bf16[16,1792]{1,0:T(8,128)(2,1)}, u32[]{:S(2)}) copy-start(bf16[16,1792]{1,0:T(8,128)(2,1)} %own_ref.1) | copy-start | bytes 172036
  12.8 22.8 %all-to-all-start = ((bf16[4,7,2,32,256]{4,3,2,1,0:T(8,128)(2,1)}), bf16[4,7,2,32,256]{4,3,2,1,0:T(8,128)(2,1)S(1)}, u32[]{:S(2)}, u32[]{:S(2)}) async-start(bf16[4,7,2,32,256]{4,3,2,1,0:T(8,128)(2,1)} %get-tuple-element.12), calls=%async_computation | async-start | bytes 1835008 | tf_op jit(solution)/shard_map/all_to_all | solution.py:217
  17.1 50.4 %collective-permute-start = (bf16[16,1792]{1,0:T(8,128)(2,1)S(1)}, bf16[16,1792]{1,0:T(8,128)(2,1)S(1)}, u32[]{:S(2)}, u32[]{:S(2)}) collective-permute-start(bf16[16,1792]{1,0:T(8,128)(2,1)S(1)} %copy-done.1), channel_id=1, source_target_pairs={{0,8},{8,0},{1,9},{9,1},{2,10},{10,2},{3,11},{11,3},{4,12},{12,4},... | collective-permute-start | bytes 172040 | tf_op jit(solution)/shard_map/ppermute | solution.py:190
  87.1 34.0 %all-to-all-start.2 = ((bf16[4,16,32,256]{3,2,1,0:T(8,128)(2,1)}), bf16[4,16,32,256]{3,2,1,0:T(8,128)(2,1)S(1)}, u32[]{:S(2)}, u32[]{:S(2)}) async-start(bf16[4,16,32,256]{3,2,1,0:T(8,128)(2,1)} %broadcast_in_dim.10), calls=%async_computation.2 | async-start | bytes 2097152 | tf_op jit(solution)/shard_map/all_to_all | solution.py:262
  117.2 22.1 %copy-start = (bf16[2048,512]{1,0:T(8,128)(2,1)S(1)}, bf16[2048,512]{1,0:T(8,128)(2,1)}, u32[]{:S(2)}) copy-start(bf16[2048,512]{1,0:T(8,128)(2,1)} %all-gather.5.cloned.1.call-done) | copy-start | bytes 6291460
Sparse Core Ops, SparseCore 0:
  12.9 54.2 all-gather.4
